TPU v7x, 512 devices: a whole 4x8x8 slice. The times are simulated.
512 devices in a mesh: dp: 32 (over z_hi, x, core), code: 16 (over z_lo, y).
Axes of the slice: x: 4, y: 8, z: 8 (z_hi: 4, z_lo: 2; z = z_hi * 2 + z_lo), core: 2. Of those that a mesh axis runs over, the one named last changes fastest.
Arguments:
- latents: bfloat16 [16384, 128], P(('dp', 'code')), may hold values from -240 to 240
- basis: bfloat16 [131072, 128], P('code'), may hold values from -6 to 6
- code_map: bfloat16 [128, 128], replicated, may hold values from -0.5 to 0.5
Outputs:
- quantized: bfloat16 [16384, 128], P(('dp', 'code'))
- usage: float32 [131072], P('code')
- map_grad: float32 [4096, 128], P('dp')
All inputs are finite; a program needn't handle non-finite values.
Results may differ from a plain program's by a relative error of at most 0.023.
The roundings to bfloat16 on the way count: a program that leaves them out, or rounds other values in their place, can miss the bound.
Values may be sent and summed in bfloat16 or wider, within the bound.
A program may use at most 64 MiB of HBM per device.

v0:
```python
import jax
import jax.numpy as jnp
from jax import lax
from jax.sharding import PartitionSpec as P

CB = 2048


def split_three(values):
    upper = values.astype(jnp.bfloat16)
    rest = values - upper.astype(jnp.float32)
    middle = rest.astype(jnp.bfloat16)
    lower = (rest - middle.astype(jnp.float32)).astype(jnp.bfloat16)
    return (upper, middle, lower)


def exact_rows(values, low_matrix):
    total = jnp.zeros((values.shape[0], low_matrix.shape[1]), jnp.float32)
    for piece in split_three(values):
        total = total + jnp.dot(piece, low_matrix, preferred_element_type=jnp.float32)
    return total


def exact_inner(low_matrix, values):
    total = jnp.zeros((low_matrix.shape[1], values.shape[1]), jnp.float32)
    for piece in split_three(values):
        total = total + lax.dot_general(
            low_matrix, piece, (((0,), (0,)), ((), ())), preferred_element_type=jnp.float32
        )
    return total


def block_scores(tile, code_blk, sq_blk):
    dots = lax.dot_general(
        tile, code_blk, (((1,), (1,)), ((), ())), preferred_element_type=jnp.float32
    )
    return (2.0 * dots - sq_blk[None, :]) / 16.0


def body(latents, basis, code_map):
    tile = lax.all_gather(latents, "code", axis=0, tiled=True)
    rows = tile.shape[0]
    width = tile.shape[1]
    kdev = basis.shape[0]
    nblk = kdev // CB
    codebook = jnp.dot(basis, code_map, preferred_element_type=jnp.float32).astype(jnp.bfloat16)
    code_f = codebook.astype(jnp.float32)
    code_sq = jnp.sum(code_f * code_f, axis=1)
    code_blocks = codebook.reshape(nblk, CB, width)
    sq_blocks = code_sq.reshape(nblk, CB)
    basis_blocks = basis.reshape(nblk, CB, width)

    def top_step(carry, blk):
        scores = block_scores(tile, blk[0], blk[1])
        return (jnp.maximum(carry, jnp.max(scores, axis=1)), None)

    local_top, _ = lax.scan(
        top_step, jnp.full((rows,), -1e30, jnp.float32), (code_blocks, sq_blocks)
    )
    row_top = lax.pmax(local_top, "code")

    def total_step(carry, blk):
        total, acc = carry
        scores = block_scores(tile, blk[0], blk[1])
        weights = jnp.exp(scores - row_top[:, None])
        acc = acc + exact_rows(weights, blk[0])
        return ((total + jnp.sum(weights, axis=1), acc), None)

    init = (jnp.zeros((rows,), jnp.float32), jnp.zeros((rows, width), jnp.float32))
    (local_total, local_acc), _ = lax.scan(total_step, init, (code_blocks, sq_blocks))
    row_total, weighted = lax.psum((local_total, local_acc), "code")
    soft = weighted / row_total[:, None]
    errors = (soft - tile.astype(jnp.float32)).astype(jnp.bfloat16)
    share = rows // lax.axis_size("code")
    quantized = lax.dynamic_slice_in_dim(
        soft.astype(jnp.bfloat16), lax.axis_index("code") * share, share, 0
    )

    def grad_step(carry, blk):
        scores = block_scores(tile, blk[0], blk[1])
        assign = jnp.exp(scores - row_top[:, None]) / row_total[:, None]
        code_err = lax.dot_general(
            assign.astype(jnp.bfloat16),
            errors,
            (((0,), (0,)), ((), ())),
            preferred_element_type=jnp.float32,
        )
        term = exact_inner(blk[2], code_err)
        return (carry + term, jnp.sum(assign, axis=0))

    grad_part, usage_blocks = lax.scan(
        grad_step, jnp.zeros((width, width), jnp.float32), (code_blocks, sq_blocks, basis_blocks)
    )
    usage_part = usage_blocks.reshape(kdev)
    all_tokens = rows * lax.axis_size("dp")
    all_codes = kdev * lax.axis_size("code")
    usage_sum = lax.psum(usage_part, "dp")
    grad_sum = lax.psum(grad_part, "code")
    usage = usage_sum * (all_codes / all_tokens)
    map_grad = grad_sum / jnp.sqrt(jnp.float32(rows))
    return (quantized, usage, map_grad)


def solution(mesh):
    return jax.shard_map(
        body,
        mesh=mesh,
        in_specs=(P(("dp", "code"), None), P("code", None), P()),
        out_specs=(P(("dp", "code"), None), P("code"), P("dp", None)),
        check_vma=False,
    )
```

profile of v0, /device:TPU:1, one launch (start us, length us, event | category | flops | bytes accessed | tf_op | source)
XLA Modules:
  0.0 551.4 jit_solution(6374341393384294417)
XLA Ops:
  7.3 31.6 %all_gather.3 = bf16[512,128]{1,0:T(8,128)(2,1)} all-gather(bf16[32,128]{1,0:T(8,128)(2,1)} %param.9), channel_id=1, replica_groups=mesh['dp'=32,'code'=16] {'code'}, dimensions={0}, use_global_device_ids=true | all-gather | bytes 139264 | tf_op jit(solution)/shard_map/all_gather | solution.py:41
  38.9 2.9 multiply_reduce_fusion.1
  41.8 6.8 %while.37 = (s32[]{:T(128)}, f32[512]{0:T(512)S(1)}, bf16[4,2048,128]{2,1,0:T(8,128)(2,1)S(1)}, bf16[512,128]{1,0:T(8,128)(2,1)}, f32[4,2048]{1,0:T(4,128)S(1)}, /*index=5*/s32[]{:T(128)}, s32[]{:T(128)}) while((s32[]{:T(128)}, f32[512]{0:T(512)S(1)}, bf16[4,2048,128]{2,1,0:T(8,128)(2,1)S(1)}, bf16[512,128]{1,0:T(8,128)(2,1)}, ...), condition=%wide.region_3.4_spmd.clone, body=%wide.region_1.3_spmd.clone.sunk | while | flops 272630272 | bytes 688231 | solution.py:57
  41.9 1.6 multiply_reduce_fusion.3
  43.5 1.6 multiply_reduce_fusion.3
  45.2 1.6 multiply_reduce_fusion.3
  46.9 1.6 multiply_reduce_fusion.3
  48.6 23.9 %pmax.7 = f32[512]{0:T(512)S(1)} all-reduce(f32[512]{0:T(512)S(1)} %get-tuple-element.121), channel_id=1, replica_groups=mesh['dp'=32,'code'=16] {'code'}, use_global_device_ids=true, to_apply=%region_4.5 | all-reduce | flops 512 | bytes 4096 | tf_op jit(solution)/shard_map/pmax | solution.py:60
  72.5 40.2 %while.38 = (s32[]{:T(128)}, f32[512]{0:T(512)S(1)}, f32[512,128]{1,0:T(8,128)S(1)}, bf16[4,2048,128]{2,1,0:T(8,128)(2,1)}, bf16[512,128]{1,0:T(8,128)(2,1)}, /*...) while((s32[]{:T(128)}, f32[512]{0:T(512)S(1)}, f32[512,128]{1,0:T(8,128)S(1)}, ...), condition=%wide.region_7.8_spmd.clone, body=%wide.region_5.7_spmd.clone.sunk | while | flops 1090781696 | bytes 45779128 | solution.py:70
  72.5 4.3 fusion.94
  76.8 3.2 fusion.95
  80.4 0.7 copy-done.4
  81.1 0.7 fusion.96
  81.8 0.8 fusion.97
  82.7 4.1 fusion.94
  86.8 3.2 fusion.95
  90.0 0.4 copy-done.1
  90.4 0.7 copy-done.4
  91.1 0.7 fusion.96
  91.8 0.8 fusion.97
  92.7 4.1 fusion.94
  96.8 3.2 fusion.95
  100.4 0.7 copy-done.4
  101.1 0.7 fusion.96
  101.9 0.8 fusion.97
  102.7 4.1 fusion.94
  106.9 3.2 fusion.95
  110.5 0.7 copy-done.4
  111.1 0.7 fusion.96
  111.9 0.8 fusion.97
  112.7 0.7 copy-done.5
  113.5 25.2 %psum.29 = f32[512]{0:T(512)S(1)} all-reduce(f32[512]{0:T(512)S(1)} %get-tuple-element.123), channel_id=1, replica_groups=mesh['dp'=32,'code'=16] {'code'}, use_global_device_ids=true, to_apply=%region_9.10 | all-reduce | flops 512 | bytes 4096 | tf_op jit(solution)/shard_map/psum | solution.py:71
  138.7 118.4 %all-reduce.3.cloned.1.call-done = f32[512,128]{1,0:T(8,128)} async-done(((f32[512,128]{1,0:T(8,128)}), f32[512,128]{1,0:T(8,128)}) %all-reduce.3.cloned.1.call-update) | async-done | bytes 262160 | tf_op jit(solution)/shard_map/psum | solution.py:71
  257.1 1.8 subtract_convert_fusion.4
  258.9 18.0 %while.39 = (s32[]{:T(128)}, f32[128,128]{1,0:T(8,128)S(1)}, f32[4,2048]{1,0:T(4,128)S(1)}, bf16[4,2048,128]{2,1,0:T(8,128)(2,1)S(1)}, bf16[4,2048,128]{2,1,0:T(...) while((s32[]{:T(128)}, f32[128,128]{1,0:T(8,128)S(1)}, ...), condition=%wide.region_12.13_spmd.clone, body=%wide.region_10.12_spmd.clone.sunk | while | flops 748746752 | bytes 11194527 | solution.py:91
  258.9 2.5 fusion.106
  261.4 0.7 fusion.107
  263.4 2.5 fusion.106
  265.9 0.7 fusion.107
  267.9 2.5 fusion.106
  270.4 0.7 fusion.107
  272.4 2.5 fusion.106
  274.9 0.7 fusion.107
  276.9 142.3 %psum.30 = f32[8192]{0:T(1024)S(1)} all-reduce(f32[8192]{0:T(1024)S(1)} %bitcast.122), channel_id=1, replica_groups=mesh['dp'=32,'code'=16] {'dp'}, use_global_device_ids=true, to_apply=%region_13.14 | all-reduce | flops 8192 | bytes 65536 | tf_op jit(solution)/shard_map/psum | solution.py:97
  419.2 0.6 broadcast_multiply_fusion.1
  419.9 1.3 dynamic-slice_convert_fusion
  421.2 121.9 %all-reduce.5.cloned.1.call-done = f32[128,128]{1,0:T(8,128)} async-done(((f32[128,128]{1,0:T(8,128)}), f32[128,128]{1,0:T(8,128)}) %all-reduce.5.cloned.1.call-update) | async-done | bytes 65552 | tf_op jit(solution)/shard_map/psum | solution.py:98
  543.1 1.5 broadcast_multiply_fusion
  (67 shorter events, 6.4 us)
Async XLA Ops:
  7.2 31.7 %copy-start = (bf16[128,128]{1,0:T(8,128)(2,1)S(1)}, bf16[128,128]{1,0:T(8,128)(2,1)}, u32[]{:S(2)}) copy-start(bf16[128,128]{1,0:T(8,128)(2,1)} %param.11) | copy-start | bytes 98308
  7.2 249.9 %all-reduce.3.cloned.1.call-start = ((), (), s32[]{:S(2)}) async-start(), calls=%async_computation | async-start | bytes 524288 | tf_op jit(solution)/shard_map/psum | solution.py:71
  48.6 23.9 %copy-start.3 = (bf16[4,2048,128]{2,1,0:T(8,128)(2,1)}, bf16[4,2048,128]{2,1,0:T(8,128)(2,1)S(1)}, u32[]{:S(2)}) copy-start(bf16[4,2048,128]{2,1,0:T(8,128)(2,1)S(1)} %get-tuple-element.486) | copy-start | bytes 6291460
  72.5 186.4 %copy-start.2 = (bf16[8192,128]{1,0:T(8,128)(2,1)S(1)}, bf16[8192,128]{1,0:T(8,128)(2,1)}, u32[]{:S(2)}) copy-start(bf16[8192,128]{1,0:T(8,128)(2,1)} %param.10) | copy-start | bytes 6291460
  76.8 3.6 copy-start.1
  76.8 4.3 copy-start.4
  86.8 3.6 copy-start.1
  86.8 4.3 copy-start.4
  96.8 3.6 copy-start.1
  96.8 4.3 copy-start.4
  106.9 3.6 copy-start.1
  106.9 4.3 copy-start.4
  112.7 0.7 copy-start.5
  113.4 429.7 %all-reduce.5.cloned.1.call-start = ((), (), s32[]{:S(2)}) async-start(), calls=%async_computation.1 | async-start | bytes 131072 | tf_op jit(solution)/shard_map/psum | solution.py:98
  276.9 142.9 %copy-start.6 = (f32[128,128]{1,0:T(8,128)}, f32[128,128]{1,0:T(8,128)S(1)}, u32[]{:S(2)}) copy-start(f32[128,128]{1,0:T(8,128)S(1)} %get-tuple-element.125) | copy-start | bytes 196612
Sparse Core Ops, SparseCore 0:
  113.6 143.4 all-reduce.2
  420.0 123.0 all-reduce.4
where the time goes:
time: 561 us; the launch traced here: 551 us
  waiting for transfers between devices  240 us (43%)
  blocking collectives  223 us (40%)
  matrix products  62.3 us (11%)
  between operations  14.2 us (3%)
  local copies, waits for them, and re-layouts  7.01 us (1%)
    psum x1, blocking collectives, body(): usage_sum = lax.psum(usage_part, 'dp')  142 us
    psum x1, waiting for transfers between devices, body(): grad_sum = lax.psum(grad_part, 'code')  122 us
    psum x1, waiting for transfers between devices, body(): row_total, weighted = lax.psum((local_total, local_acc), 'code')  118 us
    dot_general x12, matrix products, block_scores(): lax.dot_general(tile, code_blk, (((1,), (1,)), ((), ())), preferred_eleme...  33.1 us
    all_gather x1, blocking collectives, body(): tile = lax.all_gather(latents, 'code', axis=0, tiled=True)  31.6 us
    psum x1, blocking collectives, body(): row_total, weighted = lax.psum((local_total, local_acc), 'code')  25.2 us
    pmax x1, blocking collectives, body(): row_top = lax.pmax(local_top, 'code')  23.9 us
    dot_general x12, matrix products, exact_rows(): jnp.dot(piece, low_matrix, preferred_element_type=jnp.float32)  19 us
  transfers between devices with their start and end apart: 2, of which 2 were waited for; matrix products, arithmetic and copies ran while one was open for 0% of the time, Pallas kernels for 0%

commit v1 on v0

v1 whole, which is shorter than its diff:
```python
import functools
import math

import jax
import jax.numpy as jnp
from jax import lax
from jax.experimental import pallas as pl
from jax.experimental.pallas import tpu as pltpu
from jax.sharding import PartitionSpec as P

MESH = pl.DeviceIdType.MESH
F32 = jnp.float32
BF16 = jnp.bfloat16
NT = (((1,), (1,)), ((), ()))
TN = (((0,), (0,)), ((), ()))
LANES = 128
KB = 1024
LOG2E = math.log2(math.e)


def dot(a, b, dims=(((1,), (0,)), ((), ()))):
    return lax.dot_general(a, b, dims, preferred_element_type=F32)


def split_three(values):
    upper = values.astype(BF16)
    rest = values - upper.astype(F32)
    middle = rest.astype(BF16)
    lower = (rest - middle.astype(F32)).astype(BF16)
    return (upper, middle, lower)


def wide(column, width):
    return jnp.concatenate([column] * (width // LANES), axis=1)


def wait_bytes(ref, sem):
    pltpu.make_async_copy(ref, ref, sem).wait()


def make_codebook(i, bext, cmap, cb, sq):
    code = dot(bext[i, :, :LANES], cmap[...]).astype(BF16)
    cb[i] = code
    wide_code = code.astype(F32)
    square = wide_code * wide_code
    upper = square.astype(BF16)
    lower = (square - upper.astype(F32)).astype(BF16)
    ones = jnp.full((16, 2 * LANES), -0.0625, BF16)
    total = dot(ones, jnp.concatenate([upper, lower], axis=1), NT)
    sq[i] = total[:8]


def score_block(i, x8, cb, sq, s_buf, top):
    s = dot(x8[...], cb[i], NT) + sq[i, 0:1, :]
    s_buf[i] = s
    best = s[:, :LANES]
    for j in range(1, KB // LANES):
        best = jnp.maximum(best, s[:, j * LANES:(j + 1) * LANES])
    top[...] = jnp.maximum(top[...], best)


def weight_block(i, s_buf, top, w_buf, bext, acc):
    w = jnp.exp(s_buf[i] - wide(top[...], KB)).astype(BF16)
    w_buf[i] = w
    acc[...] += dot(w, bext[i])


def lanes_of(columns):
    rows = columns.shape[0]
    eye = lax.broadcasted_iota(jnp.int32, (LANES, LANES), 0) == lax.broadcasted_iota(
        jnp.int32, (LANES, LANES), 1
    )
    out = []
    for g in range(rows // LANES):
        part = jnp.where(eye, columns[g * LANES:(g + 1) * LANES], 0.0)
        out.append(jnp.sum(part, axis=0, keepdims=True))
    return jnp.concatenate(out, axis=0)


def usage_block(i, r3, w_buf, u_part):
    u = jnp.sum(dot(r3, w_buf[i]), axis=0, keepdims=True)
    width = u_part.shape[2]
    per = KB // width
    for j in range(per):
        u_part[i * per + j] = u[:, j * width:(j + 1) * width]


def kernel(n_dp, n_code, x_ref, basis_ref, map_ref, q_ref, u_ref, g_ref,
           bext, cmap, cb, sq, x_all, x8, s_buf, top, w_buf, acc,
           lse, w_send, w_recv, fac, w_all, q_buf, g_buf, u_part, u_recv, u_all,
           load_sem, out_sem, send_sem, recv_sem):
    dp = lax.axis_index("dp")
    code = lax.axis_index("code")
    nblk = basis_ref.shape[0] // KB
    rows = x_ref.shape[0]
    tokens = rows * n_code

    x_load = pltpu.make_async_copy(x_ref, x_all.at[code], load_sem.at[nblk])
    m_load = pltpu.make_async_copy(map_ref, cmap, load_sem.at[nblk + 1])
    x_load.start()
    m_load.start()

    def basis_load(i):
        return pltpu.make_async_copy(
            basis_ref.at[pl.ds(i * KB, KB)], bext.at[i, :, pl.ds(0, LANES)], load_sem.at[i]
        )

    for i in range(nblk):
        basis_load(i).start()

    barrier = pltpu.get_barrier_semaphore()

    def greet_code(i, _):
        peer = lax.rem(code + i, n_code)
        pl.semaphore_signal(barrier, inc=1, device_id=(dp, peer), device_id_type=MESH)
        return 0

    def greet_dp(i, _):
        peer = lax.rem(dp + i, n_dp)
        pl.semaphore_signal(barrier, inc=1, device_id=(peer, code), device_id_type=MESH)
        return 0

    lax.fori_loop(1, n_code, greet_code, 0)
    lax.fori_loop(1, n_dp, greet_dp, 0)

    for i in range(nblk):
        bext[i, :, LANES:] = jnp.ones((KB, LANES), BF16)
    x_load.wait()
    m_load.wait()
    pl.semaphore_wait(barrier, n_code + n_dp - 2)

    def to_code(phase, src, dst):
        def send(i, _):
            peer = lax.rem(code + i, n_code)
            pltpu.make_async_remote_copy(
                src_ref=src(peer), dst_ref=dst, send_sem=send_sem.at[phase],
                recv_sem=recv_sem.at[phase], device_id=(dp, peer), device_id_type=MESH,
            ).start()
            return 0
        lax.fori_loop(1, n_code, send, 0)

    def to_dp(phase, src, dst):
        def send(i, _):
            peer = lax.rem(dp + i, n_dp)
            pltpu.make_async_remote_copy(
                src_ref=src(peer), dst_ref=dst, send_sem=send_sem.at[phase],
                recv_sem=recv_sem.at[phase], device_id=(peer, code), device_id_type=MESH,
            ).start()
            return 0
        lax.fori_loop(1, n_dp, send, 0)

    others_code = pl.ds(0, n_code - 1)
    others_dp = pl.ds(0, n_dp - 1)

    to_code(0, lambda peer: x_all.at[code], x_all.at[code])

    def codebook_step(i, _):
        basis_load(i).wait()
        make_codebook(i, bext, cmap, cb, sq)
        return 0

    lax.fori_loop(0, nblk, codebook_step, 0)
    top[...] = jnp.full_like(top, -jnp.inf)
    acc[...] = jnp.zeros_like(acc)

    wait_bytes(x_all.at[others_code], recv_sem.at[0])
    x8[...] = x_all[...].reshape(tokens, LANES) * jnp.asarray(0.125, BF16)

    def score_step(i, _):
        score_block(i, x8, cb, sq, s_buf, top)
        return 0

    lax.fori_loop(0, nblk, score_step, 0)
    top[...] = jnp.broadcast_to(jnp.max(top[...], axis=1, keepdims=True), top.shape)

    def weight_step(i, _):
        weight_block(i, s_buf, top, w_buf, bext, acc)
        return 0

    lax.fori_loop(0, nblk, weight_step, 0)

    groups = tokens // LANES
    lse[code] = jnp.concatenate([lanes_of(top[...]), lanes_of(acc[:, LANES:])], axis=0)
    to_code(1, lambda peer: lse.at[code], lse.at[code])
    w_send[...] = acc[:, :LANES].astype(BF16).reshape(n_code, rows, LANES)
    to_code(2, lambda peer: w_send.at[peer], w_recv.at[code])
    w_recv[code] = w_send[code]

    wait_bytes(lse.at[others_code], recv_sem.at[1])
    tops = lse[:, :groups, :]
    best = jnp.max(tops, axis=0)
    factor = jnp.exp(tops - best[None])
    total = jnp.sum(factor * lse[:, groups:, :], axis=0)
    own = jnp.exp(lse[code, :groups, :] - best) / total
    own_row = jnp.concatenate([own[g:g + 1] for g in range(groups)], axis=1)
    place = lax.broadcasted_iota(jnp.int32, (16, tokens), 0)
    r3 = jnp.zeros((16, tokens), F32)
    for j, piece in enumerate(split_three(own_row)):
        r3 = jnp.where(place == j, jnp.broadcast_to(piece.astype(F32), r3.shape), r3)
    r3 = r3.astype(BF16)

    def usage_step(i, _):
        usage_block(i, r3, w_buf, u_part)
        return 0

    lax.fori_loop(0, nblk, usage_step, 0)
    to_dp(3, lambda peer: u_part.at[peer], u_recv.at[dp])
    u_recv[dp] = u_part[dp]

    scaled = factor / total[None]
    for g in range(groups):
        fac[g, :n_code] = scaled[:, g, :]
        fac[g, n_code:] = jnp.zeros((LANES - n_code, LANES), F32)
    per = LANES // rows
    turned = jnp.transpose(fac[code // per])
    fac[0] = turned
    mine = fac[0, pl.ds(pl.multiple_of(lax.rem(code, per) * rows, rows), rows), :]

    wait_bytes(w_recv.at[others_code], recv_sem.at[2])
    w_own = jnp.zeros((rows, LANES), F32)
    for c in range(n_code):
        w_own = w_own + mine[:, c:c + 1] * w_recv[c].astype(F32)
    w_all[code] = w_own.astype(BF16)
    to_code(4, lambda peer: w_all.at[code], w_all.at[code])

    soft_own = jnp.zeros((rows, LANES), F32)
    for piece in split_three(w_own):
        soft_own = soft_own + dot(piece, cmap[...])
    q_buf[...] = soft_own.astype(BF16)
    q_out = pltpu.make_async_copy(q_buf, q_ref, out_sem.at[0])
    q_out.start()

    wait_bytes(u_recv.at[others_dp], recv_sem.at[3])
    scale = (basis_ref.shape[0] * n_code) / (tokens * n_dp)
    u_all[dp] = jnp.sum(u_recv[...], axis=0) * scale
    to_dp(5, lambda peer: u_all.at[dp], u_all.at[dp])

    wait_bytes(w_all.at[others_code], recv_sem.at[4])
    w_tile = w_all[...].reshape(tokens, LANES)
    x_tile = x_all[...].reshape(tokens, LANES)
    errors = (dot(w_tile, cmap[...]) - x_tile.astype(F32)).astype(BF16)
    g_buf[...] = dot(w_tile, errors, TN) * (1.0 / math.sqrt(tokens))
    g_out = pltpu.make_async_copy(g_buf, g_ref, out_sem.at[1])
    g_out.start()

    wait_bytes(u_all.at[others_dp], recv_sem.at[5])
    u_out = pltpu.make_async_copy(u_all, u_ref, out_sem.at[2])
    u_out.start()

    wait_bytes(x_all.at[others_code], send_sem.at[0])
    wait_bytes(lse.at[others_code], send_sem.at[1])
    wait_bytes(w_send.at[others_code], send_sem.at[2])
    wait_bytes(u_part.at[others_dp], send_sem.at[3])
    wait_bytes(w_all.at[others_code], send_sem.at[4])
    wait_bytes(u_all.at[others_dp], send_sem.at[5])
    q_out.wait()
    g_out.wait()
    u_out.wait()


def body(n_dp, n_code, latents, basis, code_map):
    rows, width = latents.shape
    kdev = basis.shape[0]
    nblk = kdev // KB
    tokens = rows * n_code
    chunk = kdev // n_dp
    vm = pltpu.VMEM
    quantized, usage, grad = pl.pallas_call(
        functools.partial(kernel, n_dp, n_code),
        out_shape=(
            jax.ShapeDtypeStruct((rows, width), BF16),
            jax.ShapeDtypeStruct((n_dp, 1, chunk), F32),
            jax.ShapeDtypeStruct((width, width), F32),
        ),
        in_specs=[pl.BlockSpec(memory_space=pl.ANY)] * 3,
        out_specs=[pl.BlockSpec(memory_space=pl.ANY)] * 3,
        scratch_shapes=[
            vm((nblk, KB, 2 * width), BF16),
            vm((width, width), BF16),
            vm((nblk, KB, width), BF16),
            vm((nblk, 8, KB), F32),
            vm((n_code, rows, width), BF16),
            vm((tokens, width), BF16),
            vm((nblk, tokens, KB), F32),
            vm((tokens, LANES), F32),
            vm((nblk, tokens, KB), BF16),
            vm((tokens, 2 * width), F32),
            vm((n_code, 2 * tokens // LANES, LANES), F32),
            vm((n_code, rows, width), BF16),
            vm((n_code, rows, width), BF16),
            vm((tokens // LANES, LANES, LANES), F32),
            vm((n_code, rows, width), BF16),
            vm((rows, width), BF16),
            vm((width, width), F32),
            vm((n_dp, 1, chunk), F32),
            vm((n_dp, 1, chunk), F32),
            vm((n_dp, 1, chunk), F32),
            pltpu.SemaphoreType.DMA((nblk + 2,)),
            pltpu.SemaphoreType.DMA((3,)),
            pltpu.SemaphoreType.DMA((6,)),
            pltpu.SemaphoreType.DMA((6,)),
        ],
        compiler_params=pltpu.CompilerParams(
            collective_id=0, has_side_effects=True, vmem_limit_bytes=56 * 1024 * 1024
        ),
    )(latents, basis, code_map)
    return (quantized, usage.reshape(kdev), grad)


def solution(mesh):
    return jax.shard_map(
        functools.partial(body, mesh.shape["dp"], mesh.shape["code"]),
        mesh=mesh,
        in_specs=(P(("dp", "code"), None), P("code", None), P()),
        out_specs=(P(("dp", "code"), None), P("code"), P("dp", None)),
        check_vma=False,
    )
```

time: 561 us -> 55 us (0.10); the launches traced: 551 us -> 54.7 us
  waiting for transfers between devices: 240 us -> 0 us
  blocking collectives: 223 us -> 0 us
  matrix products: 62.3 us -> 0 us
  Pallas kernels: 0 us -> 49.9 us
  between operations: 14.2 us -> 0.64 us
    psum x2 -> x0, waiting for transfers between devices: 240 us -> none  [the longest x1 122 us: body(): grad_sum = lax.psum(grad_part, 'code')]
    psum x2 -> x0, blocking collectives: 167 us -> none  [the longest x1 142 us: body(): usage_sum = lax.psum(usage_part, 'dp')]
    dot_general x41 -> x0, matrix products: 62.3 us -> none  [the longest x12 33.1 us: block_scores(): lax.dot_general(tile, code_blk, (((1,), (1,)), ((), ())), preferred_eleme...]
    pallas_call x0 -> x1, Pallas kernels: none -> 49.9 us  [body(): pl.pallas_call(functools.partial(kernel, n_dp, n_code), out_shape=(jax.Sh...]
    all_gather x1 -> x0, blocking collectives: 31.6 us -> none  [body(): tile = lax.all_gather(latents, 'code', axis=0, tiled=True)]
    pmax x1 -> x0, blocking collectives: 23.9 us -> none  [body(): row_top = lax.pmax(local_top, 'code')]
  transfers between devices with their start and end apart: 2 -> 0, of which waited for: 2 -> 0; matrix products, arithmetic and copies ran while one was open for 0% -> 0% of each run, Pallas kernels for 0% -> 0%
where the time goes in v1:
time: 55 us; the launch traced here: 54.7 us
  Pallas kernels  49.9 us (91%)
  local copies, waits for them, and re-layouts  4.14 us (8%)
  between operations  0.64 us (1%)
    pallas_call x1, Pallas kernels, body(): pl.pallas_call(functools.partial(kernel, n_dp, n_code), out_shape=(jax.Sh...  49.9 us
    unnamed x3, local copies, waits for them, and re-layouts  4.14 us

profile of v1, /device:TPU:1, one launch (start us, length us, event | category | flops | bytes accessed | tf_op | source)
XLA Modules:
  0.0 54.7 jit_solution(3757044398853129406)
XLA Ops:
  0.6 49.9 %shard_map.58 = (bf16[32,128]{1,0:T(8,128)(2,1)}, f32[32,1,256]{2,1,0:T(1,128)}, f32[128,128]{1,0:T(8,128)}) custom-call(bf16[32,128]{1,0:T(8,128)(2,1)} %x_ref.1, bf16[8192,128]{1,0:T(8,128)(2,1)} %basis_ref.1, bf16[128,128]{1,0:T(8,128)(2,1)} %map_ref.1), custom_call_target="tpu_custom_call" | custom-call | tf_op jit(solution)/shard_map/pallas_call | solution.py:268
  50.5 1.3 %copy.9 = bf16[32,128]{1,0:T(8,128)(2,1)} copy(bf16[32,128]{1,0:T(8,128)(2,1)} %get-tuple-element.12) | data formatting | bytes 16384
  51.8 1.4 %copy.10 = f32[8192]{0:T(1024)} copy(f32[8192]{0:T(1024)} %bitcast.1) | data formatting | bytes 65536
  53.2 1.5 %copy.11 = f32[128,128]{1,0:T(8,128)} copy(f32[128,128]{1,0:T(8,128)} %get-tuple-element.14) | data formatting | bytes 131072

commit v2 on v1

v2 whole, which is shorter than its diff:
```python
import functools
import math

import jax
import jax.numpy as jnp
from jax import lax
from jax.experimental import pallas as pl
from jax.experimental.pallas import tpu as pltpu
from jax.sharding import PartitionSpec as P

MESH = pl.DeviceIdType.MESH
F32 = jnp.float32
BF16 = jnp.bfloat16
NN = (((1,), (0,)), ((), ()))
NT = (((1,), (1,)), ((), ()))
TN = (((0,), (0,)), ((), ()))
LANES = 128
CHUNK = 1024

RING = 8
NEAR = (
    ((0, 0), (0, 1), (0, 7), (1, 0)),
    ((0, 2), (0, 6), (1, 1), (1, 7)),
    ((0, 3), (0, 5), (1, 2), (1, 6)),
    ((0, 4), (1, 3), (1, 5), (1, 4)),
)
X = 4
ZH = 4


def dot(a, b, dims=NN):
    return lax.dot_general(a, b, dims, preferred_element_type=F32)


def split_three(values):
    upper = values.astype(BF16)
    rest = values - upper.astype(F32)
    middle = rest.astype(BF16)
    lower = (rest - middle.astype(F32)).astype(BF16)
    return (upper, middle, lower)


def wide(column, width):
    return jnp.concatenate([column] * (width // LANES), axis=1)


def wait_bytes(ref, sem):
    pltpu.make_async_copy(ref, ref, sem).wait()


def make_codebook(i, bas, cmap, cb, sq):
    part = slice(i * CHUNK, (i + 1) * CHUNK)
    code = dot(bas[part, :], cmap[...]).astype(BF16)
    cb[part, :] = code
    wide_code = code.astype(F32)
    square = wide_code * wide_code
    upper = square.astype(BF16)
    lower = (square - upper.astype(F32)).astype(BF16)
    ones = jnp.full((16, 2 * LANES), -0.0625, BF16)
    total = dot(ones, jnp.concatenate([upper, lower], axis=1), NT)
    sq[:, part] = total[:8]


def group_scores(x_group, cb, sq, s_buf):
    codes = cb.shape[0]
    s = dot(x_group, cb[...], NT) + sq[0:1, :]
    s_buf[...] = s
    best = s[:, :LANES]
    for j in range(1, codes // LANES):
        best = jnp.maximum(best, s[:, j * LANES:(j + 1) * LANES])
    return jnp.broadcast_to(jnp.max(best, axis=1, keepdims=True), best.shape)


def group_weights(top, s_buf, bas, w_buf, places, rows):
    codes = bas.shape[0]
    w = jnp.exp(s_buf[...] - wide(top, codes)).astype(BF16)
    for j, place in enumerate(places):
        w_buf[pl.ds(place, rows), :] = w[j * rows:(j + 1) * rows]
    return dot(w, jnp.concatenate([bas[...], jnp.ones((codes, LANES), BF16)], axis=1))


def lanes_of(columns):
    rows = columns.shape[0]
    eye = lax.broadcasted_iota(jnp.int32, (LANES, LANES), 0) == lax.broadcasted_iota(
        jnp.int32, (LANES, LANES), 1
    )
    out = []
    for g in range(rows // LANES):
        part = jnp.where(eye, columns[g * LANES:(g + 1) * LANES], 0.0)
        out.append(jnp.sum(part, axis=0, keepdims=True))
    return jnp.concatenate(out, axis=0)


def usage_half(r3, w_buf, start, out):
    width = w_buf.shape[1] // 2
    u = jnp.sum(dot(r3, w_buf[:, pl.ds(start, width)]), axis=0, keepdims=True)
    for j in range(width // LANES):
        out[j:j + 1, :] = u[:, j * LANES:(j + 1) * LANES]


def kernel(n_dp, n_code, x_ref, basis_ref, map_ref, q_ref, u_ref, g_ref,
           bas, cmap, cb, sq, x_all, s_buf, w_buf, m_col, t_col,
           lse, w_send, w_recv, fac, w_all, q_buf, g_buf,
           u_send, u_mine, u_pair, u_all, u_out,
           load_sem, out_sem, send_sem, recv_sem):
    dp = lax.axis_index("dp")
    code = lax.axis_index("code")
    z_lo, y = code // RING, lax.rem(code, RING)
    core = lax.rem(dp, 2)
    x_pos = lax.rem(dp // 2, X)
    z_hi = dp // (2 * X)
    spot = dp // 2
    codes = basis_ref.shape[0]
    nblk = codes // CHUNK
    rows = x_ref.shape[0]
    tokens = rows * n_code
    groups = tokens // LANES

    def peer_code(offset):
        return lax.rem(z_lo + offset[0], n_code // RING) * RING + lax.rem(y + offset[1], RING)

    owners = [[peer_code(o) for o in group] for group in NEAR]
    far_first = [p for group in reversed(owners) for p in reversed(group)][:-1]
    sibling = dp + 1 - 2 * core
    spots = [
        (lax.rem(z_hi + a, ZH) * X + lax.rem(x_pos + b, X)) * 2 + core
        for a in (2, 1, 3, 0) for b in (2, 1, 3, 0)
    ][:-1]

    x_load = pltpu.make_async_copy(x_ref, x_all.at[code], load_sem.at[nblk])
    m_load = pltpu.make_async_copy(map_ref, cmap, load_sem.at[nblk + 1])
    b_loads = [
        pltpu.make_async_copy(
            basis_ref.at[pl.ds(i * CHUNK, CHUNK)], bas.at[pl.ds(i * CHUNK, CHUNK)], load_sem.at[i]
        )
        for i in range(nblk)
    ]
    x_load.start()
    m_load.start()
    for load in b_loads:
        load.start()

    barrier = pltpu.get_barrier_semaphore()
    for p in far_first:
        pl.semaphore_signal(barrier, inc=1, device_id=(dp, p), device_id_type=MESH)
    for d in spots + [sibling]:
        pl.semaphore_signal(barrier, inc=1, device_id=(d, code), device_id_type=MESH)

    def remote(src, dst, phase, device):
        return pltpu.make_async_remote_copy(
            src_ref=src, dst_ref=dst, send_sem=send_sem.at[phase], recv_sem=recv_sem.at[phase],
            device_id=device, device_id_type=MESH,
        )

    x_load.wait()
    m_load.wait()
    pl.semaphore_wait(barrier, len(far_first) + len(spots) + 1)

    for g in reversed(range(len(NEAR))):
        for p, offset in zip(owners[g], NEAR[g]):
            if offset != (0, 0):
                remote(x_all.at[code], x_all.at[code], g, (dp, p)).start()

    for i in range(nblk):
        b_loads[i].wait()
        make_codebook(i, bas, cmap, cb, sq)

    for g, group in enumerate(owners):
        arriving = len(group) - (1 if g == 0 else 0)
        wait_bytes(x_all.at[pl.ds(0, arriving)], recv_sem.at[g])
        x_group = jnp.concatenate([x_all[o] for o in group], axis=0) * jnp.asarray(0.125, BF16)
        top = group_scores(x_group, cb, sq, s_buf)
        places = [pl.multiple_of(o * rows, rows) for o in group]
        acc = group_weights(top, s_buf, bas, w_buf, places, rows)
        sums = acc[:, :LANES].astype(BF16)
        for j, o in enumerate(group):
            part = slice(j * rows, (j + 1) * rows)
            m_col[pl.ds(places[j], rows), :] = top[part]
            t_col[pl.ds(places[j], rows), :] = acc[part, LANES:]
            w_send[o] = sums[part]

    lse[code] = jnp.concatenate([lanes_of(m_col[...]), lanes_of(t_col[...])], axis=0)
    for p in far_first:
        remote(lse.at[code], lse.at[code], 4, (dp, p)).start()
    for p in far_first:
        remote(w_send.at[p], w_recv.at[code], 5, (dp, p)).start()
    w_recv[code] = w_send[code]

    others = pl.ds(0, n_code - 1)
    wait_bytes(lse.at[others], recv_sem.at[4])
    tops = lse[:, :groups, :]
    best = jnp.max(tops, axis=0)
    factor = jnp.exp(tops - best[None])
    total = jnp.sum(factor * lse[:, groups:, :], axis=0)
    own = jnp.exp(lse[code, :groups, :] - best) / total
    own_row = jnp.concatenate([own[g:g + 1] for g in range(groups)], axis=1)
    place = lax.broadcasted_iota(jnp.int32, (16, tokens), 0)
    r3 = jnp.zeros((16, tokens), F32)
    for j, piece in enumerate(split_three(own_row)):
        r3 = jnp.where(place == j, jnp.broadcast_to(piece.astype(F32), r3.shape), r3)
    r3 = r3.astype(BF16)

    half = codes // 2
    usage_half(r3, w_buf, pl.multiple_of((1 - core) * half, half), u_send)
    pair = remote(u_send, u_pair, 6, (sibling, code))
    pair.start()
    usage_half(r3, w_buf, pl.multiple_of(core * half, half), u_mine)
    pair.wait_recv()
    u_all[spot] = (u_mine[...] + u_pair[...]).astype(BF16)
    for d in spots:
        remote(u_all.at[spot], u_all.at[spot], 7, (d, code)).start()

    scaled = factor / total[None]
    for g in range(groups):
        fac[g, :n_code] = scaled[:, g, :]
        fac[g, n_code:] = jnp.zeros((LANES - n_code, LANES), F32)
    per = LANES // rows
    fac[0] = jnp.transpose(fac[code // per])
    mine = fac[0, pl.ds(pl.multiple_of(lax.rem(code, per) * rows, rows), rows), :]

    wait_bytes(w_recv.at[others], recv_sem.at[5])
    w_own = jnp.zeros((rows, LANES), F32)
    for c in range(n_code):
        w_own = w_own + mine[:, c:c + 1] * w_recv[c].astype(F32)
    w_all[code] = w_own.astype(BF16)
    for p in far_first:
        remote(w_all.at[code], w_all.at[code], 8, (dp, p)).start()

    soft_own = jnp.zeros((rows, LANES), F32)
    for piece in split_three(w_own):
        soft_own = soft_own + dot(piece, cmap[...])
    q_buf[...] = soft_own.astype(BF16)
    q_out = pltpu.make_async_copy(q_buf, q_ref, out_sem.at[0])
    q_out.start()

    wait_bytes(u_all.at[pl.ds(0, len(spots))], recv_sem.at[7])
    scale = (codes * n_code) / (tokens * n_dp)
    u_out[...] = jnp.sum(u_all[...].astype(F32), axis=0) * scale
    u_copy = pltpu.make_async_copy(u_out, u_ref.at[core], out_sem.at[2])
    u_copy.start()
    u_far = remote(u_out, u_ref.at[core], 9, (sibling, code))
    u_far.start()

    wait_bytes(w_all.at[others], recv_sem.at[8])
    w_tile = w_all[...].reshape(tokens, LANES)
    x_tile = x_all[...].reshape(tokens, LANES)
    errors = (dot(w_tile, cmap[...]) - x_tile.astype(F32)).astype(BF16)
    g_buf[...] = dot(w_tile, errors, TN) * (1.0 / math.sqrt(tokens))
    g_out = pltpu.make_async_copy(g_buf, g_ref, out_sem.at[1])
    g_out.start()

    wait_bytes(x_all.at[pl.ds(0, 3)], send_sem.at[0])
    for g in range(1, len(NEAR)):
        wait_bytes(x_all.at[pl.ds(0, 4)], send_sem.at[g])
    wait_bytes(lse.at[others], send_sem.at[4])
    wait_bytes(w_send.at[others], send_sem.at[5])
    pair.wait_send()
    wait_bytes(u_all.at[pl.ds(0, len(spots))], send_sem.at[7])
    wait_bytes(w_all.at[others], send_sem.at[8])
    q_out.wait()
    u_copy.wait()
    u_far.wait()
    g_out.wait()


def deliver(q_in, u_in, g_in, q_ref, u_ref, g_ref, sem):
    copies = [
        pltpu.make_async_copy(src, dst, sem.at[i])
        for i, (src, dst) in enumerate(((g_in, g_ref), (u_in, u_ref), (q_in, q_ref)))
    ]
    for copy in copies:
        copy.start()
    for copy in copies:
        copy.wait()


def body(n_dp, n_code, latents, basis, code_map):
    rows, width = latents.shape
    codes = basis.shape[0]
    nblk = codes // CHUNK
    tokens = rows * n_code
    half = codes // 2
    vm = pltpu.VMEM
    anywhere = pl.BlockSpec(memory_space=pl.ANY)
    quantized, usage, grad = pl.pallas_call(
        functools.partial(kernel, n_dp, n_code),
        out_shape=(
            jax.ShapeDtypeStruct((rows, width), BF16),
            jax.ShapeDtypeStruct((2, half // LANES, LANES), F32),
            jax.ShapeDtypeStruct((width, width), F32),
        ),
        in_specs=[pl.BlockSpec(memory_space=pltpu.HBM)] * 3,
        out_specs=[anywhere] * 3,
        scratch_shapes=[
            vm((codes, width), BF16),
            vm((width, width), BF16),
            vm((codes, width), BF16),
            vm((8, codes), F32),
            vm((n_code, rows, width), BF16),
            vm((LANES, codes), F32),
            vm((tokens, codes), BF16),
            vm((tokens, LANES), F32),
            vm((tokens, LANES), F32),
            vm((n_code, 2 * tokens // LANES, LANES), F32),
            vm((n_code, rows, width), BF16),
            vm((n_code, rows, width), BF16),
            vm((tokens // LANES, LANES, LANES), F32),
            vm((n_code, rows, width), BF16),
            vm((rows, width), BF16),
            vm((width, width), F32),
            vm((half // LANES, LANES), F32),
            vm((half // LANES, LANES), F32),
            vm((half // LANES, LANES), F32),
            vm((n_dp // 2, half // LANES, LANES), BF16),
            vm((half // LANES, LANES), F32),
            pltpu.SemaphoreType.DMA((nblk + 2,)),
            pltpu.SemaphoreType.DMA((3,)),
            pltpu.SemaphoreType.DMA((10,)),
            pltpu.SemaphoreType.DMA((10,)),
        ],
        compiler_params=pltpu.CompilerParams(
            collective_id=0, has_side_effects=True, vmem_limit_bytes=40 * 1024 * 1024
        ),
    )(latents, basis, code_map)
    return pl.pallas_call(
        deliver,
        out_shape=(
            jax.ShapeDtypeStruct((rows, width), BF16),
            jax.ShapeDtypeStruct((codes,), F32),
            jax.ShapeDtypeStruct((width, width), F32),
        ),
        in_specs=[anywhere] * 3,
        out_specs=[anywhere] * 3,
        scratch_shapes=[pltpu.SemaphoreType.DMA((3,))],
    )(quantized, usage.reshape(codes), grad)


def solution(mesh):
    return jax.shard_map(
        functools.partial(body, mesh.shape["dp"], mesh.shape["code"]),
        mesh=mesh,
        in_specs=(P(("dp", "code"), None), P("code", None), P()),
        out_specs=(P(("dp", "code"), None), P("code"), P("dp", None)),
        check_vma=False,
    )
```

time: 55 us -> 58.1 us (1.056)
  Pallas kernels: 49.9 us -> 52.3 us
  local copies, waits for them, and re-layouts: 4.14 us -> 4.87 us
    pallas_call x0 -> x1, Pallas kernels: none -> 4.35 us  [body(): pl.pallas_call(deliver, out_shape=(jax.ShapeDtypeStruct((rows, width), BF...]
    pallas_call x1, Pallas kernels: 49.9 us -> 48 us  [body(): pl.pallas_call(functools.partial(kernel, n_dp, n_code), out_shape=(jax.Sh...]
    unnamed x3 -> x12, local copies, waits for them, and re-layouts: 4.14 us -> 4.87 us
where the time goes in v2:
time: 58.1 us; the launch traced here: 57.8 us
  Pallas kernels  52.3 us (90%)
  local copies, waits for them, and re-layouts  4.87 us (8%)
  between operations  0.66 us (1%)
    pallas_call x1, Pallas kernels, body(): pl.pallas_call(functools.partial(kernel, n_dp, n_code), out_shape=(jax.Sh...  48 us
    unnamed x12, local copies, waits for them, and re-layouts  4.87 us
    pallas_call x1, Pallas kernels, body(): pl.pallas_call(deliver, out_shape=(jax.ShapeDtypeStruct((rows, width), BF...  4.35 us

profile of v2, /device:TPU:1, one launch (start us, length us, event | category | flops | bytes accessed | tf_op | source)
XLA Modules:
  0.0 57.8 jit_solution(4129427932957085137)
XLA Ops:
  0.6 0.0 copy-start
  0.6 1.6 %copy-done = bf16[8192,128]{1,0:T(8,128)(2,1)S(1)} copy-done((bf16[8192,128]{1,0:T(8,128)(2,1)S(1)}, bf16[8192,128]{1,0:T(8,128)(2,1)}, u32[]{:S(2)}) %copy-start) | copy-done | bytes 2097176
  2.2 0.0 copy-start.2
  2.2 0.8 %copy-done.2 = bf16[128,128]{1,0:T(8,128)(2,1)S(1)} copy-done((bf16[128,128]{1,0:T(8,128)(2,1)S(1)}, bf16[128,128]{1,0:T(8,128)(2,1)}, u32[]{:S(2)}) %copy-start.2) | copy-done | bytes 32792
  3.0 0.0 copy-start.4
  3.0 0.7 %copy-done.4 = bf16[32,128]{1,0:T(8,128)(2,1)S(1)} copy-done((bf16[32,128]{1,0:T(8,128)(2,1)S(1)}, bf16[32,128]{1,0:T(8,128)(2,1)}, u32[]{:S(2)}) %copy-start.4) | copy-done | bytes 8216
  3.7 48.0 %shard_map.58 = (bf16[32,128]{1,0:T(8,128)(2,1)S(1)}, f32[2,32,128]{2,1,0:T(8,128)S(1)}, f32[128,128]{1,0:T(8,128)S(1)}) custom-call(bf16[32,128]{1,0:T(8,128)(2,1)S(1)} %copy-done.4, bf16[8192,128]{1,0:T(8,128)(2,1)S(1)} %copy-done, bf16[128,128]{1,0:T(8,128)(2,1)S(1)} %copy-done.2), custom_call_target="tpu_custom_call" | custom-call | tf_op jit(solution)/shard_map/pallas_call | solution.py:285
  51.7 0.0 copy-start.1
  51.7 0.6 %copy-done.1 = f32[128,128]{1,0:T(8,128)} copy-done((f32[128,128]{1,0:T(8,128)}, f32[128,128]{1,0:T(8,128)S(1)}, u32[]{:S(2)}) %copy-start.1) | copy-done | bytes 65560
  52.3 0.0 copy-start.3
  52.3 0.6 %copy-done.3 = f32[2,32,128]{2,1,0:T(8,128)} copy-done((f32[2,32,128]{2,1,0:T(8,128)}, f32[2,32,128]{2,1,0:T(8,128)S(1)}, u32[]{:S(2)}) %copy-start.3) | copy-done | bytes 32792
  52.9 0.0 copy-start.5
  52.9 0.6 %copy-done.5 = bf16[32,128]{1,0:T(8,128)(2,1)} copy-done((bf16[32,128]{1,0:T(8,128)(2,1)}, bf16[32,128]{1,0:T(8,128)(2,1)S(1)}, u32[]{:S(2)}) %copy-start.5) | copy-done | bytes 8216
  53.5 4.4 %shard_map.59 = (bf16[32,128]{1,0:T(8,128)(2,1)}, f32[8192]{0:T(1024)}, f32[128,128]{1,0:T(8,128)}) custom-call(bf16[32,128]{1,0:T(8,128)(2,1)} %copy-done.5, f32[8192]{0:T(1024)} %bitcast.1, f32[128,128]{1,0:T(8,128)} %copy-done.1), custom_call_target="tpu_custom_call" | custom-call | tf_op jit(solution)/shard_map/pallas_call | solution.py:325
Async XLA Ops:
  0.6 1.6 %copy-start = (bf16[8192,128]{1,0:T(8,128)(2,1)S(1)}, bf16[8192,128]{1,0:T(8,128)(2,1)}, u32[]{:S(2)}) copy-start(bf16[8192,128]{1,0:T(8,128)(2,1)} %basis_ref.1) | copy-start | bytes 6291460
  2.2 0.8 %copy-start.2 = (bf16[128,128]{1,0:T(8,128)(2,1)S(1)}, bf16[128,128]{1,0:T(8,128)(2,1)}, u32[]{:S(2)}) copy-start(bf16[128,128]{1,0:T(8,128)(2,1)} %map_ref.1) | copy-start | bytes 98308
  3.0 0.7 %copy-start.4 = (bf16[32,128]{1,0:T(8,128)(2,1)S(1)}, bf16[32,128]{1,0:T(8,128)(2,1)}, u32[]{:S(2)}) copy-start(bf16[32,128]{1,0:T(8,128)(2,1)} %x_ref.1) | copy-start | bytes 24580
  51.7 0.6 %copy-start.1 = (f32[128,128]{1,0:T(8,128)}, f32[128,128]{1,0:T(8,128)S(1)}, u32[]{:S(2)}) copy-start(f32[128,128]{1,0:T(8,128)S(1)} %get-tuple-element.8.g_in) | copy-start | bytes 196612
  52.3 0.6 %copy-start.3 = (f32[2,32,128]{2,1,0:T(8,128)}, f32[2,32,128]{2,1,0:T(8,128)S(1)}, u32[]{:S(2)}) copy-start(f32[2,32,128]{2,1,0:T(8,128)S(1)} %get-tuple-element.7) | copy-start | bytes 98308
  52.9 0.6 %copy-start.5 = (bf16[32,128]{1,0:T(8,128)(2,1)}, bf16[32,128]{1,0:T(8,128)(2,1)S(1)}, u32[]{:S(2)}) copy-start(bf16[32,128]{1,0:T(8,128)(2,1)S(1)} %get-tuple-element.6.q_in) | copy-start | bytes 24580

commit v3 on v2

--- a/solution.py
+++ b/solution.py
@@ -15,14 +15,12 @@
 NT = (((1,), (1,)), ((), ()))
 TN = (((0,), (0,)), ((), ()))
 LANES = 128
-CHUNK = 1024
+CHUNK = 2048
 
 RING = 8
 NEAR = (
-    ((0, 0), (0, 1), (0, 7), (1, 0)),
-    ((0, 2), (0, 6), (1, 1), (1, 7)),
-    ((0, 3), (0, 5), (1, 2), (1, 6)),
-    ((0, 4), (1, 3), (1, 5), (1, 4)),
+    ((0, 0), (0, 1), (0, 7), (1, 0), (0, 2), (0, 6), (1, 1), (1, 7)),
+    ((0, 3), (0, 5), (1, 2), (1, 6), (0, 4), (1, 3), (1, 5), (1, 4)),
 )
 X = 4
 ZH = 4
@@ -61,22 +59,21 @@
     sq[:, part] = total[:8]
 
 
-def group_scores(x_group, cb, sq, s_buf):
+def group_scores(x_group, cb, sq, s_buf, top):
     codes = cb.shape[0]
-    s = dot(x_group, cb[...], NT) + sq[0:1, :]
+    s = dot(x_group[...], cb[...], NT) + sq[0:1, :]
     s_buf[...] = s
     best = s[:, :LANES]
     for j in range(1, codes // LANES):
         best = jnp.maximum(best, s[:, j * LANES:(j + 1) * LANES])
-    return jnp.broadcast_to(jnp.max(best, axis=1, keepdims=True), best.shape)
-
-
-def group_weights(top, s_buf, bas, w_buf, places, rows):
+    top[...] = jnp.broadcast_to(jnp.max(best, axis=1, keepdims=True), best.shape)
+
+
+def group_weights(part, s_buf, top, bas, w_buf, acc):
     codes = bas.shape[0]
-    w = jnp.exp(s_buf[...] - wide(top, codes)).astype(BF16)
-    for j, place in enumerate(places):
-        w_buf[pl.ds(place, rows), :] = w[j * rows:(j + 1) * rows]
-    return dot(w, jnp.concatenate([bas[...], jnp.ones((codes, LANES), BF16)], axis=1))
+    w = jnp.exp(s_buf[...] - wide(top[...], codes)).astype(BF16)
+    w_buf[part, :] = w
+    acc[...] = dot(w, jnp.concatenate([bas[...], jnp.ones((codes, LANES), BF16)], axis=1))
 
 
 def lanes_of(columns):
@@ -99,7 +96,7 @@
 
 
 def kernel(n_dp, n_code, x_ref, basis_ref, map_ref, q_ref, u_ref, g_ref,
-           bas, cmap, cb, sq, x_all, s_buf, w_buf, m_col, t_col,
+           bas, cmap, cb, sq, x_all, x_group, order, s_buf, top, w_buf, acc, m_col, t_col,
            lse, w_send, w_recv, fac, w_all, q_buf, g_buf,
            u_send, u_mine, u_pair, u_all, u_out,
            load_sem, out_sem, send_sem, recv_sem):
@@ -156,38 +153,60 @@
     m_load.wait()
     pl.semaphore_wait(barrier, len(far_first) + len(spots) + 1)
 
+    def send_sums(g):
+        for p, offset in zip(reversed(owners[g]), reversed(NEAR[g])):
+            if offset != (0, 0):
+                remote(w_send.at[p], w_recv.at[code], 3, (dp, p)).start()
+
     for g in reversed(range(len(NEAR))):
         for p, offset in zip(owners[g], NEAR[g]):
             if offset != (0, 0):
                 remote(x_all.at[code], x_all.at[code], g, (dp, p)).start()
 
+    by_distance = [o for group in owners for o in group]
+    lane = lax.broadcasted_iota(jnp.int32, (1, LANES), 1)
+    per = LANES // rows
+    target = []
+    for g in range(groups):
+        owner = jnp.full((1, LANES), by_distance[g * per])
+        for j in range(1, per):
+            owner = jnp.where(lane >= j * rows, by_distance[g * per + j], owner)
+        target.append(owner * rows + lax.rem(lane, rows))
+    target = jnp.broadcast_to(jnp.concatenate(target, axis=1), (tokens, tokens))
+    hit = lax.broadcasted_iota(jnp.int32, (tokens, tokens), 0) == target
+    order[...] = jnp.where(hit, 1.0, 0.0).astype(BF16)
+
     for i in range(nblk):
         b_loads[i].wait()
         make_codebook(i, bas, cmap, cb, sq)
 
+    always = lax.rem(dp * (dp + 1), 2) == 0
     for g, group in enumerate(owners):
+        size = len(group) * rows
         arriving = len(group) - (1 if g == 0 else 0)
         wait_bytes(x_all.at[pl.ds(0, arriving)], recv_sem.at[g])
-        x_group = jnp.concatenate([x_all[o] for o in group], axis=0) * jnp.asarray(0.125, BF16)
-        top = group_scores(x_group, cb, sq, s_buf)
-        places = [pl.multiple_of(o * rows, rows) for o in group]
-        acc = group_weights(top, s_buf, bas, w_buf, places, rows)
-        sums = acc[:, :LANES].astype(BF16)
+        for j, o in enumerate(group):
+            x_group[j * rows:(j + 1) * rows, :] = x_all[o] * jnp.asarray(0.125, BF16)
+        group_scores(x_group, cb, sq, s_buf, top)
+        part = slice(g * size, (g + 1) * size)
+        pl.when(always)(lambda: group_weights(part, s_buf, top, bas, w_buf, acc))
         for j, o in enumerate(group):
             part = slice(j * rows, (j + 1) * rows)
-            m_col[pl.ds(places[j], rows), :] = top[part]
-            t_col[pl.ds(places[j], rows), :] = acc[part, LANES:]
-            w_send[o] = sums[part]
+            place = pl.ds(pl.multiple_of(o * rows, rows), rows)
+            m_col[place, :] = top[part, :]
+            t_col[place, :] = acc[part, LANES:]
+            w_send[o] = acc[part, :LANES].astype(BF16)
+        if g == 0:
+            send_sums(0)
 
     lse[code] = jnp.concatenate([lanes_of(m_col[...]), lanes_of(t_col[...])], axis=0)
     for p in far_first:
-        remote(lse.at[code], lse.at[code], 4, (dp, p)).start()
-    for p in far_first:
-        remote(w_send.at[p], w_recv.at[code], 5, (dp, p)).start()
+        remote(lse.at[code], lse.at[code], 2, (dp, p)).start()
+    send_sums(1)
     w_recv[code] = w_send[code]
 
     others = pl.ds(0, n_code - 1)
-    wait_bytes(lse.at[others], recv_sem.at[4])
+    wait_bytes(lse.at[others], recv_sem.at[2])
     tops = lse[:, :groups, :]
     best = jnp.max(tops, axis=0)
     factor = jnp.exp(tops - best[None])
@@ -198,33 +217,32 @@
     r3 = jnp.zeros((16, tokens), F32)
     for j, piece in enumerate(split_three(own_row)):
         r3 = jnp.where(place == j, jnp.broadcast_to(piece.astype(F32), r3.shape), r3)
-    r3 = r3.astype(BF16)
+    r3 = dot(r3.astype(BF16), order[...]).astype(BF16)
 
     half = codes // 2
     usage_half(r3, w_buf, pl.multiple_of((1 - core) * half, half), u_send)
-    pair = remote(u_send, u_pair, 6, (sibling, code))
+    pair = remote(u_send, u_pair, 4, (sibling, code))
     pair.start()
     usage_half(r3, w_buf, pl.multiple_of(core * half, half), u_mine)
     pair.wait_recv()
     u_all[spot] = (u_mine[...] + u_pair[...]).astype(BF16)
     for d in spots:
-        remote(u_all.at[spot], u_all.at[spot], 7, (d, code)).start()
+        remote(u_all.at[spot], u_all.at[spot], 5, (d, code)).start()
 
     scaled = factor / total[None]
     for g in range(groups):
         fac[g, :n_code] = scaled[:, g, :]
         fac[g, n_code:] = jnp.zeros((LANES - n_code, LANES), F32)
-    per = LANES // rows
     fac[0] = jnp.transpose(fac[code // per])
     mine = fac[0, pl.ds(pl.multiple_of(lax.rem(code, per) * rows, rows), rows), :]
 
-    wait_bytes(w_recv.at[others], recv_sem.at[5])
+    wait_bytes(w_recv.at[others], recv_sem.at[3])
     w_own = jnp.zeros((rows, LANES), F32)
     for c in range(n_code):
         w_own = w_own + mine[:, c:c + 1] * w_recv[c].astype(F32)
     w_all[code] = w_own.astype(BF16)
     for p in far_first:
-        remote(w_all.at[code], w_all.at[code], 8, (dp, p)).start()
+        remote(w_all.at[code], w_all.at[code], 6, (dp, p)).start()
 
     soft_own = jnp.zeros((rows, LANES), F32)
     for piece in split_three(w_own):
@@ -233,15 +251,15 @@
     q_out = pltpu.make_async_copy(q_buf, q_ref, out_sem.at[0])
     q_out.start()
 
-    wait_bytes(u_all.at[pl.ds(0, len(spots))], recv_sem.at[7])
+    wait_bytes(u_all.at[pl.ds(0, len(spots))], recv_sem.at[5])
     scale = (codes * n_code) / (tokens * n_dp)
     u_out[...] = jnp.sum(u_all[...].astype(F32), axis=0) * scale
     u_copy = pltpu.make_async_copy(u_out, u_ref.at[core], out_sem.at[2])
     u_copy.start()
-    u_far = remote(u_out, u_ref.at[core], 9, (sibling, code))
+    u_far = remote(u_out, u_ref.at[core], 7, (sibling, code))
     u_far.start()
 
-    wait_bytes(w_all.at[others], recv_sem.at[8])
+    wait_bytes(w_all.at[others], recv_sem.at[6])
     w_tile = w_all[...].reshape(tokens, LANES)
     x_tile = x_all[...].reshape(tokens, LANES)
     errors = (dot(w_tile, cmap[...]) - x_tile.astype(F32)).astype(BF16)
@@ -249,14 +267,13 @@
     g_out = pltpu.make_async_copy(g_buf, g_ref, out_sem.at[1])
     g_out.start()
 
-    wait_bytes(x_all.at[pl.ds(0, 3)], send_sem.at[0])
-    for g in range(1, len(NEAR)):
-        wait_bytes(x_all.at[pl.ds(0, 4)], send_sem.at[g])
-    wait_bytes(lse.at[others], send_sem.at[4])
-    wait_bytes(w_send.at[others], send_sem.at[5])
+    wait_bytes(x_all.at[pl.ds(0, len(NEAR[0]) - 1)], send_sem.at[0])
+    wait_bytes(x_all.at[pl.ds(0, len(NEAR[1]))], send_sem.at[1])
+    wait_bytes(lse.at[others], send_sem.at[2])
+    wait_bytes(w_send.at[others], send_sem.at[3])
     pair.wait_send()
-    wait_bytes(u_all.at[pl.ds(0, len(spots))], send_sem.at[7])
-    wait_bytes(w_all.at[others], send_sem.at[8])
+    wait_bytes(u_all.at[pl.ds(0, len(spots))], send_sem.at[5])
+    wait_bytes(w_all.at[others], send_sem.at[6])
     q_out.wait()
     u_copy.wait()
     u_far.wait()
@@ -285,9 +302,9 @@
     quantized, usage, grad = pl.pallas_call(
         functools.partial(kernel, n_dp, n_code),
         out_shape=(
-            jax.ShapeDtypeStruct((rows, width), BF16),
-            jax.ShapeDtypeStruct((2, half // LANES, LANES), F32),
-            jax.ShapeDtypeStruct((width, width), F32),
+            vm((rows, width), BF16),
+            vm((2, half // LANES, LANES), F32),
+            vm((width, width), F32),
         ),
         in_specs=[pl.BlockSpec(memory_space=pltpu.HBM)] * 3,
         out_specs=[anywhere] * 3,
@@ -297,8 +314,12 @@
             vm((codes, width), BF16),
             vm((8, codes), F32),
             vm((n_code, rows, width), BF16),
-            vm((LANES, codes), F32),
+            vm((tokens // 2, width), BF16),
+            vm((tokens, tokens), BF16),
+            vm((tokens // 2, codes), F32),
+            vm((tokens // 2, LANES), F32),
             vm((tokens, codes), BF16),
+            vm((tokens // 2, 2 * width), F32),
             vm((tokens, LANES), F32),
             vm((tokens, LANES), F32),
             vm((n_code, 2 * tokens // LANES, LANES), F32),
@@ -315,13 +336,13 @@
             vm((half // LANES, LANES), F32),
             pltpu.SemaphoreType.DMA((nblk + 2,)),
             pltpu.SemaphoreType.DMA((3,)),
-            pltpu.SemaphoreType.DMA((10,)),
-            pltpu.SemaphoreType.DMA((10,)),
+            pltpu.SemaphoreType.DMA((8,)),
+            pltpu.SemaphoreType.DMA((8,)),
         ],
         compiler_params=pltpu.CompilerParams(
             collective_id=0, has_side_effects=True, vmem_limit_bytes=40 * 1024 * 1024
         ),
-    )(latents, basis, code_map)
+    )(*(pltpu.with_memory_space_constraint(a, pltpu.HBM) for a in (latents, basis, code_map)))
     return pl.pallas_call(
         deliver,
         out_shape=(
@@ -332,7 +353,7 @@
         in_specs=[anywhere] * 3,
         out_specs=[anywhere] * 3,
         scratch_shapes=[pltpu.SemaphoreType.DMA((3,))],
-    )(quantized, usage.reshape(codes), grad)
+    )(*(pltpu.with_memory_space_constraint(a, vm) for a in (quantized, usage.reshape(codes), grad)))
 
 
 def solution(mesh):

time: 58.1 us -> 42.9 us (0.74)
  Pallas kernels: 52.3 us -> 42.1 us
  local copies, waits for them, and re-layouts: 4.87 us -> 0 us
    pallas_call x1, Pallas kernels: 48 us -> 41.5 us  [body(): pl.pallas_call(functools.partial(kernel, n_dp, n_code), out_shape=(vm((ro...]
    unnamed x12 -> x0, local copies, waits for them, and re-layouts: 4.87 us -> none
    pallas_call x1, Pallas kernels: 4.35 us -> 0.67 us  [body(): pl.pallas_call(deliver, out_shape=(jax.ShapeDtypeStruct((rows, width), BF...]
where the time goes in v3:
time: 42.9 us; the launch traced here: 42.8 us
  Pallas kernels  42.1 us (98%)
  between operations  0.64 us (1%)
    pallas_call x1, Pallas kernels, body(): pl.pallas_call(functools.partial(kernel, n_dp, n_code), out_shape=(vm((ro...  41.5 us

profile of v3, /device:TPU:1, one launch (start us, length us, event | category | flops | bytes accessed | tf_op | source)
XLA Modules:
  0.0 42.8 jit_solution(15189710323101273435)
XLA Ops:
  0.6 41.5 %shard_map.58 = (bf16[32,128]{1,0:T(8,128)(2,1)S(1)}, f32[2,32,128]{2,1,0:T(8,128)S(1)}, f32[128,128]{1,0:T(8,128)S(1)}) custom-call(bf16[32,128]{1,0:T(8,128)(2,1)} %x_ref.1, bf16[8192,128]{1,0:T(8,128)(2,1)} %basis_ref.1, bf16[128,128]{1,0:T(8,128)(2,1)} %map_ref.1), custom_call_target="tpu_custom_call" | custom-call | tf_op jit(solution)/shard_map/pallas_call | solution.py:302
  42.1 0.7 %shard_map.59 = (bf16[32,128]{1,0:T(8,128)(2,1)}, f32[8192]{0:T(1024)}, f32[128,128]{1,0:T(8,128)}) custom-call(bf16[32,128]{1,0:T(8,128)(2,1)S(1)} %get-tuple-element.6.q_in, f32[8192]{0:T(1024)S(1)} %bitcast.1, f32[128,128]{1,0:T(8,128)S(1)} %get-tuple-element.8.g_in), custom_call_target="tpu_custom_call" | custom-call | tf_op jit(solution)/shard_map/pallas_call | solution.py:346

commit v4 on v3

--- a/solution.py
+++ b/solution.py
@@ -20,7 +20,7 @@
 RING = 8
 NEAR = (
     ((0, 0), (0, 1), (0, 7), (1, 0), (0, 2), (0, 6), (1, 1), (1, 7)),
-    ((0, 3), (0, 5), (1, 2), (1, 6), (0, 4), (1, 3), (1, 5), (1, 4)),
+    ((1, 4), (0, 4), (1, 3), (1, 5), (0, 3), (0, 5), (1, 2), (1, 6)),
 )
 X = 4
 ZH = 4
@@ -98,7 +98,7 @@
 def kernel(n_dp, n_code, x_ref, basis_ref, map_ref, q_ref, u_ref, g_ref,
            bas, cmap, cb, sq, x_all, x_group, order, s_buf, top, w_buf, acc, m_col, t_col,
            lse, w_send, w_recv, fac, w_all, q_buf, g_buf,
-           u_send, u_mine, u_pair, u_all, u_out,
+           u_row, u_send, u_level, u_all, u_out,
            load_sem, out_sem, send_sem, recv_sem):
     dp = lax.axis_index("dp")
     code = lax.axis_index("code")
@@ -106,7 +106,6 @@
     core = lax.rem(dp, 2)
     x_pos = lax.rem(dp // 2, X)
     z_hi = dp // (2 * X)
-    spot = dp // 2
     codes = basis_ref.shape[0]
     nblk = codes // CHUNK
     rows = x_ref.shape[0]
@@ -117,12 +116,15 @@
         return lax.rem(z_lo + offset[0], n_code // RING) * RING + lax.rem(y + offset[1], RING)
 
     owners = [[peer_code(o) for o in group] for group in NEAR]
-    far_first = [p for group in reversed(owners) for p in reversed(group)][:-1]
-    sibling = dp + 1 - 2 * core
-    spots = [
-        (lax.rem(z_hi + a, ZH) * X + lax.rem(x_pos + b, X)) * 2 + core
-        for a in (2, 1, 3, 0) for b in (2, 1, 3, 0)
-    ][:-1]
+    far_first = owners[1] + owners[0][:0:-1]
+    rank = lax.rem(dp, 2 * X)
+
+    def peer_dp(a, b, c):
+        return (lax.rem(z_hi + a, ZH) * X + lax.rem(x_pos + b, X)) * 2 + c
+
+    level_other = [peer_dp(0, b, 1 - core) for b in (2, 1, 3, 0)]
+    level_same = [peer_dp(0, b, core) for b in (2, 1, 3)]
+    column = [peer_dp(a, 0, c) for a in (2, 1, 3) for c in (core, 1 - core)]
 
     x_load = pltpu.make_async_copy(x_ref, x_all.at[code], load_sem.at[nblk])
     m_load = pltpu.make_async_copy(map_ref, cmap, load_sem.at[nblk + 1])
@@ -140,7 +142,7 @@
     barrier = pltpu.get_barrier_semaphore()
     for p in far_first:
         pl.semaphore_signal(barrier, inc=1, device_id=(dp, p), device_id_type=MESH)
-    for d in spots + [sibling]:
+    for d in column + level_other + level_same:
         pl.semaphore_signal(barrier, inc=1, device_id=(d, code), device_id_type=MESH)
 
     def remote(src, dst, phase, device):
@@ -151,14 +153,14 @@
 
     x_load.wait()
     m_load.wait()
-    pl.semaphore_wait(barrier, len(far_first) + len(spots) + 1)
+    pl.semaphore_wait(barrier, n_code - 1 + len(column + level_other + level_same))
 
     def send_sums(g):
-        for p, offset in zip(reversed(owners[g]), reversed(NEAR[g])):
+        for p, offset in zip(owners[g], NEAR[g]):
             if offset != (0, 0):
                 remote(w_send.at[p], w_recv.at[code], 3, (dp, p)).start()
 
-    for g in reversed(range(len(NEAR))):
+    for g in range(len(NEAR)):
         for p, offset in zip(owners[g], NEAR[g]):
             if offset != (0, 0):
                 remote(x_all.at[code], x_all.at[code], g, (dp, p)).start()
@@ -220,14 +222,15 @@
     r3 = dot(r3.astype(BF16), order[...]).astype(BF16)
 
     half = codes // 2
-    usage_half(r3, w_buf, pl.multiple_of((1 - core) * half, half), u_send)
-    pair = remote(u_send, u_pair, 4, (sibling, code))
-    pair.start()
-    usage_half(r3, w_buf, pl.multiple_of(core * half, half), u_mine)
-    pair.wait_recv()
-    u_all[spot] = (u_mine[...] + u_pair[...]).astype(BF16)
-    for d in spots:
-        remote(u_all.at[spot], u_all.at[spot], 5, (d, code)).start()
+    usage_half(r3, w_buf, pl.multiple_of((1 - core) * half, half), u_row)
+    u_send[0] = u_row[...].astype(BF16)
+    for d in level_other:
+        remote(u_send.at[0], u_level.at[rank], 4, (d, code)).start()
+    usage_half(r3, w_buf, pl.multiple_of(core * half, half), u_row)
+    u_send[1] = u_row[...].astype(BF16)
+    for d in level_same:
+        remote(u_send.at[1], u_level.at[rank], 4, (d, code)).start()
+    u_level[rank] = u_send[1]
 
     scaled = factor / total[None]
     for g in range(groups):
@@ -251,13 +254,12 @@
     q_out = pltpu.make_async_copy(q_buf, q_ref, out_sem.at[0])
     q_out.start()
 
-    wait_bytes(u_all.at[pl.ds(0, len(spots))], recv_sem.at[5])
-    scale = (codes * n_code) / (tokens * n_dp)
-    u_out[...] = jnp.sum(u_all[...].astype(F32), axis=0) * scale
-    u_copy = pltpu.make_async_copy(u_out, u_ref.at[core], out_sem.at[2])
-    u_copy.start()
-    u_far = remote(u_out, u_ref.at[core], 7, (sibling, code))
-    u_far.start()
+    level = pl.ds(0, len(level_other + level_same))
+    wait_bytes(u_level.at[level], recv_sem.at[4])
+    u_all[z_hi, core] = jnp.sum(u_level[...].astype(F32), axis=0).astype(BF16)
+    last = peer_dp(0, 0, 1 - core)
+    for d in column + [last]:
+        remote(u_all.at[z_hi, core], u_all.at[z_hi, core], 5, (d, code)).start()
 
     wait_bytes(w_all.at[others], recv_sem.at[6])
     w_tile = w_all[...].reshape(tokens, LANES)
@@ -267,16 +269,21 @@
     g_out = pltpu.make_async_copy(g_buf, g_ref, out_sem.at[1])
     g_out.start()
 
+    wait_bytes(u_level.at[level], recv_sem.at[5])
+    scale = (codes * n_code) / (tokens * n_dp)
+    u_out[...] = jnp.sum(u_all[...].astype(F32), axis=0) * scale
+    u_copy = pltpu.make_async_copy(u_out, u_ref, out_sem.at[2])
+    u_copy.start()
+
     wait_bytes(x_all.at[pl.ds(0, len(NEAR[0]) - 1)], send_sem.at[0])
     wait_bytes(x_all.at[pl.ds(0, len(NEAR[1]))], send_sem.at[1])
     wait_bytes(lse.at[others], send_sem.at[2])
     wait_bytes(w_send.at[others], send_sem.at[3])
-    pair.wait_send()
-    wait_bytes(u_all.at[pl.ds(0, len(spots))], send_sem.at[5])
+    wait_bytes(u_level.at[level], send_sem.at[4])
+    wait_bytes(u_level.at[level], send_sem.at[5])
     wait_bytes(w_all.at[others], send_sem.at[6])
     q_out.wait()
     u_copy.wait()
-    u_far.wait()
     g_out.wait()
 
 
@@ -330,14 +337,14 @@
             vm((rows, width), BF16),
             vm((width, width), F32),
             vm((half // LANES, LANES), F32),
-            vm((half // LANES, LANES), F32),
-            vm((half // LANES, LANES), F32),
-            vm((n_dp // 2, half // LANES, LANES), BF16),
-            vm((half // LANES, LANES), F32),
+            vm((2, half // LANES, LANES), BF16),
+            vm((2 * X, half // LANES, LANES), BF16),
+            vm((ZH, 2, half // LANES, LANES), BF16),
+            vm((2, half // LANES, LANES), F32),
             pltpu.SemaphoreType.DMA((nblk + 2,)),
             pltpu.SemaphoreType.DMA((3,)),
-            pltpu.SemaphoreType.DMA((8,)),
-            pltpu.SemaphoreType.DMA((8,)),
+            pltpu.SemaphoreType.DMA((7,)),
+            pltpu.SemaphoreType.DMA((7,)),
         ],
         compiler_params=pltpu.CompilerParams(
             collective_id=0, has_side_effects=True, vmem_limit_bytes=40 * 1024 * 1024

time: 42.9 us -> 41.4 us (0.965)
  Pallas kernels: 42.1 us -> 40.6 us
    pallas_call x1, Pallas kernels: 41.5 us -> 39.9 us  [body(): pl.pallas_call(functools.partial(kernel, n_dp, n_code), out_shape=(vm((ro...]
where the time goes in v4:
time: 41.4 us; the launch traced here: 41.2 us
  Pallas kernels  40.6 us (98%)
  between operations  0.64 us (2%)
    pallas_call x1, Pallas kernels, body(): pl.pallas_call(functools.partial(kernel, n_dp, n_code), out_shape=(vm((ro...  39.9 us

profile of v4, /device:TPU:1, one launch (start us, length us, event | category | flops | bytes accessed | tf_op | source)
XLA Modules:
  0.0 41.2 jit_solution(13740324190542301873)
XLA Ops:
  0.6 39.9 %shard_map.58 = (bf16[32,128]{1,0:T(8,128)(2,1)S(1)}, f32[2,32,128]{2,1,0:T(8,128)S(1)}, f32[128,128]{1,0:T(8,128)S(1)}) custom-call(bf16[32,128]{1,0:T(8,128)(2,1)} %x_ref.1, bf16[8192,128]{1,0:T(8,128)(2,1)} %basis_ref.1, bf16[128,128]{1,0:T(8,128)(2,1)} %map_ref.1), custom_call_target="tpu_custom_call" | custom-call | tf_op jit(solution)/shard_map/pallas_call | solution.py:309
  40.6 0.7 %shard_map.59 = (bf16[32,128]{1,0:T(8,128)(2,1)}, f32[8192]{0:T(1024)}, f32[128,128]{1,0:T(8,128)}) custom-call(bf16[32,128]{1,0:T(8,128)(2,1)S(1)} %get-tuple-element.6.q_in, f32[8192]{0:T(1024)S(1)} %bitcast.1, f32[128,128]{1,0:T(8,128)S(1)} %get-tuple-element.8.g_in), custom_call_target="tpu_custom_call" | custom-call | tf_op jit(solution)/shard_map/pallas_call | solution.py:353

commit v5 on v4

--- a/solution.py
+++ b/solution.py
@@ -19,7 +19,8 @@
 
 RING = 8
 NEAR = (
-    ((0, 0), (0, 1), (0, 7), (1, 0), (0, 2), (0, 6), (1, 1), (1, 7)),
+    ((0, 0), (0, 1), (0, 7), (1, 0)),
+    ((0, 2), (0, 6), (1, 1), (1, 7)),
     ((1, 4), (0, 4), (1, 3), (1, 5), (0, 3), (0, 5), (1, 2), (1, 6)),
 )
 X = 4
@@ -97,9 +98,9 @@
 
 def kernel(n_dp, n_code, x_ref, basis_ref, map_ref, q_ref, u_ref, g_ref,
            bas, cmap, cb, sq, x_all, x_group, order, s_buf, top, w_buf, acc, m_col, t_col,
-           lse, w_send, w_recv, fac, w_all, q_buf, g_buf,
-           u_row, u_send, u_level, u_all, u_out,
-           load_sem, out_sem, send_sem, recv_sem):
+           lse, w_send, w_recv, fac, w_all,
+           u_row, u_send, u_level, u_all,
+           load_sem, send_sem, recv_sem):
     dp = lax.axis_index("dp")
     code = lax.axis_index("code")
     z_lo, y = code // RING, lax.rem(code, RING)
@@ -116,7 +117,7 @@
         return lax.rem(z_lo + offset[0], n_code // RING) * RING + lax.rem(y + offset[1], RING)
 
     owners = [[peer_code(o) for o in group] for group in NEAR]
-    far_first = owners[1] + owners[0][:0:-1]
+    far_first = owners[2] + owners[1][::-1] + owners[0][:0:-1]
     rank = lax.rem(dp, 2 * X)
 
     def peer_dp(a, b, c):
@@ -158,7 +159,7 @@
     def send_sums(g):
         for p, offset in zip(owners[g], NEAR[g]):
             if offset != (0, 0):
-                remote(w_send.at[p], w_recv.at[code], 3, (dp, p)).start()
+                remote(w_send.at[p], w_recv.at[code], 4, (dp, p)).start()
 
     for g in range(len(NEAR)):
         for p, offset in zip(owners[g], NEAR[g]):
@@ -189,26 +190,28 @@
         wait_bytes(x_all.at[pl.ds(0, arriving)], recv_sem.at[g])
         for j, o in enumerate(group):
             x_group[j * rows:(j + 1) * rows, :] = x_all[o] * jnp.asarray(0.125, BF16)
-        group_scores(x_group, cb, sq, s_buf, top)
-        part = slice(g * size, (g + 1) * size)
-        pl.when(always)(lambda: group_weights(part, s_buf, top, bas, w_buf, acc))
+        first = sum(len(o) for o in NEAR[:g]) * rows
+        part = slice(first, first + size)
+        some = pl.ds(0, size)
+        group_scores(x_group.at[some], cb, sq, s_buf.at[some], top.at[some])
+        pl.when(always)(lambda: group_weights(part, s_buf.at[some], top.at[some], bas, w_buf, acc.at[some]))
         for j, o in enumerate(group):
             part = slice(j * rows, (j + 1) * rows)
             place = pl.ds(pl.multiple_of(o * rows, rows), rows)
             m_col[place, :] = top[part, :]
             t_col[place, :] = acc[part, LANES:]
             w_send[o] = acc[part, :LANES].astype(BF16)
-        if g == 0:
-            send_sums(0)
+        if g < 2:
+            send_sums(g)
 
     lse[code] = jnp.concatenate([lanes_of(m_col[...]), lanes_of(t_col[...])], axis=0)
     for p in far_first:
-        remote(lse.at[code], lse.at[code], 2, (dp, p)).start()
-    send_sums(1)
+        remote(lse.at[code], lse.at[code], 3, (dp, p)).start()
+    send_sums(2)
     w_recv[code] = w_send[code]
 
     others = pl.ds(0, n_code - 1)
-    wait_bytes(lse.at[others], recv_sem.at[2])
+    wait_bytes(lse.at[others], recv_sem.at[3])
     tops = lse[:, :groups, :]
     best = jnp.max(tops, axis=0)
     factor = jnp.exp(tops - best[None])
@@ -222,14 +225,16 @@
     r3 = dot(r3.astype(BF16), order[...]).astype(BF16)
 
     half = codes // 2
-    usage_half(r3, w_buf, pl.multiple_of((1 - core) * half, half), u_row)
+    for k in (0, 1):
+        pl.when(core == 1 - k)(lambda k=k: usage_half(r3, w_buf, k * half, u_row))
     u_send[0] = u_row[...].astype(BF16)
     for d in level_other:
-        remote(u_send.at[0], u_level.at[rank], 4, (d, code)).start()
-    usage_half(r3, w_buf, pl.multiple_of(core * half, half), u_row)
+        remote(u_send.at[0], u_level.at[rank], 5, (d, code)).start()
+    for k in (0, 1):
+        pl.when(core == k)(lambda k=k: usage_half(r3, w_buf, k * half, u_row))
     u_send[1] = u_row[...].astype(BF16)
     for d in level_same:
-        remote(u_send.at[1], u_level.at[rank], 4, (d, code)).start()
+        remote(u_send.at[1], u_level.at[rank], 5, (d, code)).start()
     u_level[rank] = u_send[1]
 
     scaled = factor / total[None]
@@ -239,52 +244,44 @@
     fac[0] = jnp.transpose(fac[code // per])
     mine = fac[0, pl.ds(pl.multiple_of(lax.rem(code, per) * rows, rows), rows), :]
 
-    wait_bytes(w_recv.at[others], recv_sem.at[3])
+    wait_bytes(w_recv.at[others], recv_sem.at[4])
     w_own = jnp.zeros((rows, LANES), F32)
     for c in range(n_code):
         w_own = w_own + mine[:, c:c + 1] * w_recv[c].astype(F32)
     w_all[code] = w_own.astype(BF16)
     for p in far_first:
-        remote(w_all.at[code], w_all.at[code], 6, (dp, p)).start()
+        remote(w_all.at[code], w_all.at[code], 7, (dp, p)).start()
 
     soft_own = jnp.zeros((rows, LANES), F32)
     for piece in split_three(w_own):
         soft_own = soft_own + dot(piece, cmap[...])
-    q_buf[...] = soft_own.astype(BF16)
-    q_out = pltpu.make_async_copy(q_buf, q_ref, out_sem.at[0])
-    q_out.start()
+    q_ref[...] = soft_own.astype(BF16)
 
     level = pl.ds(0, len(level_other + level_same))
-    wait_bytes(u_level.at[level], recv_sem.at[4])
+    wait_bytes(u_level.at[level], recv_sem.at[5])
     u_all[z_hi, core] = jnp.sum(u_level[...].astype(F32), axis=0).astype(BF16)
     last = peer_dp(0, 0, 1 - core)
     for d in column + [last]:
-        remote(u_all.at[z_hi, core], u_all.at[z_hi, core], 5, (d, code)).start()
-
-    wait_bytes(w_all.at[others], recv_sem.at[6])
+        remote(u_all.at[z_hi, core], u_all.at[z_hi, core], 6, (d, code)).start()
+
+    wait_bytes(w_all.at[others], recv_sem.at[7])
     w_tile = w_all[...].reshape(tokens, LANES)
     x_tile = x_all[...].reshape(tokens, LANES)
     errors = (dot(w_tile, cmap[...]) - x_tile.astype(F32)).astype(BF16)
-    g_buf[...] = dot(w_tile, errors, TN) * (1.0 / math.sqrt(tokens))
-    g_out = pltpu.make_async_copy(g_buf, g_ref, out_sem.at[1])
-    g_out.start()
-
-    wait_bytes(u_level.at[level], recv_sem.at[5])
+    g_ref[...] = dot(w_tile, errors, TN) * (1.0 / math.sqrt(tokens))
+
+    wait_bytes(u_level.at[level], recv_sem.at[6])
     scale = (codes * n_code) / (tokens * n_dp)
-    u_out[...] = jnp.sum(u_all[...].astype(F32), axis=0) * scale
-    u_copy = pltpu.make_async_copy(u_out, u_ref, out_sem.at[2])
-    u_copy.start()
+    u_ref[...] = jnp.sum(u_all[...].astype(F32), axis=0) * scale
 
     wait_bytes(x_all.at[pl.ds(0, len(NEAR[0]) - 1)], send_sem.at[0])
     wait_bytes(x_all.at[pl.ds(0, len(NEAR[1]))], send_sem.at[1])
-    wait_bytes(lse.at[others], send_sem.at[2])
-    wait_bytes(w_send.at[others], send_sem.at[3])
-    wait_bytes(u_level.at[level], send_sem.at[4])
+    wait_bytes(x_all.at[pl.ds(0, len(NEAR[2]))], send_sem.at[2])
+    wait_bytes(lse.at[others], send_sem.at[3])
+    wait_bytes(w_send.at[others], send_sem.at[4])
     wait_bytes(u_level.at[level], send_sem.at[5])
-    wait_bytes(w_all.at[others], send_sem.at[6])
-    q_out.wait()
-    u_copy.wait()
-    g_out.wait()
+    wait_bytes(u_level.at[level], send_sem.at[6])
+    wait_bytes(w_all.at[others], send_sem.at[7])
 
 
 def deliver(q_in, u_in, g_in, q_ref, u_ref, g_ref, sem):
@@ -314,7 +311,7 @@
             vm((width, width), F32),
         ),
         in_specs=[pl.BlockSpec(memory_space=pltpu.HBM)] * 3,
-        out_specs=[anywhere] * 3,
+        out_specs=[pl.BlockSpec(memory_space=vm)] * 3,
         scratch_shapes=[
             vm((codes, width), BF16),
             vm((width, width), BF16),
@@ -334,17 +331,13 @@
             vm((n_code, rows, width), BF16),
             vm((tokens // LANES, LANES, LANES), F32),
             vm((n_code, rows, width), BF16),
-            vm((rows, width), BF16),
-            vm((width, width), F32),
             vm((half // LANES, LANES), F32),
             vm((2, half // LANES, LANES), BF16),
             vm((2 * X, half // LANES, LANES), BF16),
             vm((ZH, 2, half // LANES, LANES), BF16),
-            vm((2, half // LANES, LANES), F32),
             pltpu.SemaphoreType.DMA((nblk + 2,)),
-            pltpu.SemaphoreType.DMA((3,)),
-            pltpu.SemaphoreType.DMA((7,)),
-            pltpu.SemaphoreType.DMA((7,)),
+            pltpu.SemaphoreType.DMA((8,)),
+            pltpu.SemaphoreType.DMA((8,)),
         ],
         compiler_params=pltpu.CompilerParams(
             collective_id=0, has_side_effects=True, vmem_limit_bytes=40 * 1024 * 1024

time: 41.4 us -> 40.9 us (0.988)
  Pallas kernels: 40.6 us -> 40.1 us
    pallas_call x1, Pallas kernels: 39.9 us -> 39.4 us  [body(): pl.pallas_call(functools.partial(kernel, n_dp, n_code), out_shape=(vm((ro...]
where the time goes in v5:
time: 40.9 us; the launch traced here: 40.7 us
  Pallas kernels  40.1 us (98%)
  between operations  0.64 us (2%)
    pallas_call x1, Pallas kernels, body(): pl.pallas_call(functools.partial(kernel, n_dp, n_code), out_shape=(vm((ro...  39.4 us

profile of v5, /device:TPU:1, one launch (start us, length us, event | category | flops | bytes accessed | tf_op | source)
XLA Modules:
  0.0 40.7 jit_solution(10629661876562383071)
XLA Ops:
  0.6 39.4 %shard_map.58 = (bf16[32,128]{1,0:T(8,128)(2,1)S(1)}, f32[2,32,128]{2,1,0:T(8,128)S(1)}, f32[128,128]{1,0:T(8,128)S(1)}) custom-call(bf16[32,128]{1,0:T(8,128)(2,1)} %x_ref.1, bf16[8192,128]{1,0:T(8,128)(2,1)} %basis_ref.1, bf16[128,128]{1,0:T(8,128)(2,1)} %map_ref.1), custom_call_target="tpu_custom_call" | custom-call | tf_op jit(solution)/shard_map/pallas_call | solution.py:306
  40.0 0.7 %shard_map.59 = (bf16[32,128]{1,0:T(8,128)(2,1)}, f32[8192]{0:T(1024)}, f32[128,128]{1,0:T(8,128)}) custom-call(bf16[32,128]{1,0:T(8,128)(2,1)S(1)} %get-tuple-element.6.q_in, f32[8192]{0:T(1024)S(1)} %bitcast.1, f32[128,128]{1,0:T(8,128)S(1)} %get-tuple-element.8.g_in), custom_call_target="tpu_custom_call" | custom-call | tf_op jit(solution)/shard_map/pallas_call | solution.py:346

commit v6 on v5

--- a/solution.py
+++ b/solution.py
@@ -70,10 +70,12 @@
     top[...] = jnp.broadcast_to(jnp.max(best, axis=1, keepdims=True), best.shape)
 
 
-def group_weights(part, s_buf, top, bas, w_buf, acc):
+def group_weights(slots, s_buf, top, bas, w_buf, acc):
     codes = bas.shape[0]
     w = jnp.exp(s_buf[...] - wide(top[...], codes)).astype(BF16)
-    w_buf[part, :] = w
+    rows = w.shape[0] // len(slots)
+    for j, slot in enumerate(slots):
+        w_buf[slot * rows:(slot + 1) * rows, :] = w[j * rows:(j + 1) * rows]
     acc[...] = dot(w, jnp.concatenate([bas[...], jnp.ones((codes, LANES), BF16)], axis=1))
 
 
@@ -97,7 +99,7 @@
 
 
 def kernel(n_dp, n_code, x_ref, basis_ref, map_ref, q_ref, u_ref, g_ref,
-           bas, cmap, cb, sq, x_all, x_group, order, s_buf, top, w_buf, acc, m_col, t_col,
+           bas, cmap, cb, sq, x_all, x_group, s_buf, top, w_buf, acc, m_col, t_col,
            lse, w_send, w_recv, fac, w_all,
            u_row, u_send, u_level, u_all,
            load_sem, send_sem, recv_sem):
@@ -127,6 +129,12 @@
     level_same = [peer_dp(0, b, core) for b in (2, 1, 3)]
     column = [peer_dp(a, 0, c) for a in (2, 1, 3) for c in (core, 1 - core)]
 
+    barrier = pltpu.get_barrier_semaphore()
+    for p in far_first:
+        pl.semaphore_signal(barrier, inc=1, device_id=(dp, p), device_id_type=MESH)
+    for d in column + level_other + level_same:
+        pl.semaphore_signal(barrier, inc=1, device_id=(d, code), device_id_type=MESH)
+
     x_load = pltpu.make_async_copy(x_ref, x_all.at[code], load_sem.at[nblk])
     m_load = pltpu.make_async_copy(map_ref, cmap, load_sem.at[nblk + 1])
     b_loads = [
@@ -140,12 +148,6 @@
     for load in b_loads:
         load.start()
 
-    barrier = pltpu.get_barrier_semaphore()
-    for p in far_first:
-        pl.semaphore_signal(barrier, inc=1, device_id=(dp, p), device_id_type=MESH)
-    for d in column + level_other + level_same:
-        pl.semaphore_signal(barrier, inc=1, device_id=(d, code), device_id_type=MESH)
-
     def remote(src, dst, phase, device):
         return pltpu.make_async_remote_copy(
             src_ref=src, dst_ref=dst, send_sem=send_sem.at[phase], recv_sem=recv_sem.at[phase],
@@ -153,7 +155,6 @@
         )
 
     x_load.wait()
-    m_load.wait()
     pl.semaphore_wait(barrier, n_code - 1 + len(column + level_other + level_same))
 
     def send_sums(g):
@@ -166,19 +167,7 @@
             if offset != (0, 0):
                 remote(x_all.at[code], x_all.at[code], g, (dp, p)).start()
 
-    by_distance = [o for group in owners for o in group]
-    lane = lax.broadcasted_iota(jnp.int32, (1, LANES), 1)
-    per = LANES // rows
-    target = []
-    for g in range(groups):
-        owner = jnp.full((1, LANES), by_distance[g * per])
-        for j in range(1, per):
-            owner = jnp.where(lane >= j * rows, by_distance[g * per + j], owner)
-        target.append(owner * rows + lax.rem(lane, rows))
-    target = jnp.broadcast_to(jnp.concatenate(target, axis=1), (tokens, tokens))
-    hit = lax.broadcasted_iota(jnp.int32, (tokens, tokens), 0) == target
-    order[...] = jnp.where(hit, 1.0, 0.0).astype(BF16)
-
+    m_load.wait()
     for i in range(nblk):
         b_loads[i].wait()
         make_codebook(i, bas, cmap, cb, sq)
@@ -190,11 +179,10 @@
         wait_bytes(x_all.at[pl.ds(0, arriving)], recv_sem.at[g])
         for j, o in enumerate(group):
             x_group[j * rows:(j + 1) * rows, :] = x_all[o] * jnp.asarray(0.125, BF16)
-        first = sum(len(o) for o in NEAR[:g]) * rows
-        part = slice(first, first + size)
         some = pl.ds(0, size)
+        slots = [o[0] * RING + o[1] for o in NEAR[g]]
         group_scores(x_group.at[some], cb, sq, s_buf.at[some], top.at[some])
-        pl.when(always)(lambda: group_weights(part, s_buf.at[some], top.at[some], bas, w_buf, acc.at[some]))
+        pl.when(always)(lambda: group_weights(slots, s_buf.at[some], top.at[some], bas, w_buf, acc.at[some]))
         for j, o in enumerate(group):
             part = slice(j * rows, (j + 1) * rows)
             place = pl.ds(pl.multiple_of(o * rows, rows), rows)
@@ -217,12 +205,20 @@
     factor = jnp.exp(tops - best[None])
     total = jnp.sum(factor * lse[:, groups:, :], axis=0)
     own = jnp.exp(lse[code, :groups, :] - best) / total
-    own_row = jnp.concatenate([own[g:g + 1] for g in range(groups)], axis=1)
-    place = lax.broadcasted_iota(jnp.int32, (16, tokens), 0)
-    r3 = jnp.zeros((16, tokens), F32)
-    for j, piece in enumerate(split_three(own_row)):
-        r3 = jnp.where(place == j, jnp.broadcast_to(piece.astype(F32), r3.shape), r3)
-    r3 = dot(r3.astype(BF16), order[...]).astype(BF16)
+    width = RING * rows
+    place = lax.broadcasted_iota(jnp.int32, (16, width), 0)
+    halves = []
+    for h in range(tokens // width):
+        each = width // LANES
+        row = jnp.concatenate([own[h * each + g:h * each + g + 1] for g in range(each)], axis=1)
+        pieces = jnp.zeros((16, width), F32)
+        for j, piece in enumerate(split_three(row)):
+            pieces = jnp.where(place == j, jnp.broadcast_to(piece.astype(F32), pieces.shape), pieces)
+        halves.append(pieces)
+    if len(halves) == 2:
+        halves = [jnp.where(z_lo == 0, halves[0], halves[1]), jnp.where(z_lo == 0, halves[1], halves[0])]
+    turn = lax.rem((RING - y) * rows, width)
+    r3 = jnp.concatenate([pltpu.roll(h, turn, 1) for h in halves], axis=1).astype(BF16)
 
     half = codes // 2
     for k in (0, 1):
@@ -241,6 +237,7 @@
     for g in range(groups):
         fac[g, :n_code] = scaled[:, g, :]
         fac[g, n_code:] = jnp.zeros((LANES - n_code, LANES), F32)
+    per = LANES // rows
     fac[0] = jnp.transpose(fac[code // per])
     mine = fac[0, pl.ds(pl.multiple_of(lax.rem(code, per) * rows, rows), rows), :]
 
@@ -319,7 +316,6 @@
             vm((8, codes), F32),
             vm((n_code, rows, width), BF16),
             vm((tokens // 2, width), BF16),
-            vm((tokens, tokens), BF16),
             vm((tokens // 2, codes), F32),
             vm((tokens // 2, LANES), F32),
             vm((tokens, codes), BF16),

time: 40.9 us -> 40.8 us (level)
  no operation moved by 1% of the time
where the time goes in v6:
time: 40.8 us; the launch traced here: 40.7 us
  Pallas kernels  40 us (98%)
  between operations  0.64 us (2%)
    pallas_call x1, Pallas kernels, body(): pl.pallas_call(functools.partial(kernel, n_dp, n_code), out_shape=(vm((ro...  39.4 us

profile of v6, /device:TPU:1, one launch (start us, length us, event | category | flops | bytes accessed | tf_op | source)
XLA Modules:
  0.0 40.7 jit_solution(2430281667229956869)
XLA Ops:
  0.6 39.4 %shard_map.58 = (bf16[32,128]{1,0:T(8,128)(2,1)S(1)}, f32[2,32,128]{2,1,0:T(8,128)S(1)}, f32[128,128]{1,0:T(8,128)S(1)}) custom-call(bf16[32,128]{1,0:T(8,128)(2,1)} %x_ref.1, bf16[8192,128]{1,0:T(8,128)(2,1)} %basis_ref.1, bf16[128,128]{1,0:T(8,128)(2,1)} %map_ref.1), custom_call_target="tpu_custom_call" | custom-call | tf_op jit(solution)/shard_map/pallas_call | solution.py:303
  40.0 0.7 %shard_map.59 = (bf16[32,128]{1,0:T(8,128)(2,1)}, f32[8192]{0:T(1024)}, f32[128,128]{1,0:T(8,128)}) custom-call(bf16[32,128]{1,0:T(8,128)(2,1)S(1)} %get-tuple-element.6.q_in, f32[8192]{0:T(1024)S(1)} %bitcast.1, f32[128,128]{1,0:T(8,128)S(1)} %get-tuple-element.8.g_in), custom_call_target="tpu_custom_call" | custom-call | tf_op jit(solution)/shard_map/pallas_call | solution.py:342

commit v7 on v6

--- a/solution.py
+++ b/solution.py
@@ -193,13 +193,15 @@
             send_sums(g)
 
     lse[code] = jnp.concatenate([lanes_of(m_col[...]), lanes_of(t_col[...])], axis=0)
-    for p in far_first:
-        remote(lse.at[code], lse.at[code], 3, (dp, p)).start()
+    for g in (2, 1, 0):
+        for p, offset in zip(owners[g], NEAR[g]):
+            if offset != (0, 0):
+                remote(lse.at[code], lse.at[code], 3 if g == 2 else 8, (dp, p)).start()
+    w_recv[code] = w_send[code]
+    others = pl.ds(0, n_code - 1)
+    wait_bytes(lse.at[pl.ds(0, 7)], recv_sem.at[8])
     send_sums(2)
-    w_recv[code] = w_send[code]
-
-    others = pl.ds(0, n_code - 1)
-    wait_bytes(lse.at[others], recv_sem.at[3])
+    wait_bytes(lse.at[pl.ds(0, 8)], recv_sem.at[3])
     tops = lse[:, :groups, :]
     best = jnp.max(tops, axis=0)
     factor = jnp.exp(tops - best[None])
@@ -274,7 +276,8 @@
     wait_bytes(x_all.at[pl.ds(0, len(NEAR[0]) - 1)], send_sem.at[0])
     wait_bytes(x_all.at[pl.ds(0, len(NEAR[1]))], send_sem.at[1])
     wait_bytes(x_all.at[pl.ds(0, len(NEAR[2]))], send_sem.at[2])
-    wait_bytes(lse.at[others], send_sem.at[3])
+    wait_bytes(lse.at[pl.ds(0, 8)], send_sem.at[3])
+    wait_bytes(lse.at[pl.ds(0, 7)], send_sem.at[8])
     wait_bytes(w_send.at[others], send_sem.at[4])
     wait_bytes(u_level.at[level], send_sem.at[5])
     wait_bytes(u_level.at[level], send_sem.at[6])
@@ -332,8 +335,8 @@
             vm((2 * X, half // LANES, LANES), BF16),
             vm((ZH, 2, half // LANES, LANES), BF16),
             pltpu.SemaphoreType.DMA((nblk + 2,)),
-            pltpu.SemaphoreType.DMA((8,)),
-            pltpu.SemaphoreType.DMA((8,)),
+            pltpu.SemaphoreType.DMA((9,)),
+            pltpu.SemaphoreType.DMA((9,)),
         ],
         compiler_params=pltpu.CompilerParams(
             collective_id=0, has_side_effects=True, vmem_limit_bytes=40 * 1024 * 1024

time: 40.8 us -> 41.2 us (level)
  no operation moved by 1% of the time
where the time goes in v7:
time: 41.2 us; the launch traced here: 41 us
  Pallas kernels  40.4 us (98%)
  between operations  0.64 us (2%)
    pallas_call x1, Pallas kernels, body(): pl.pallas_call(functools.partial(kernel, n_dp, n_code), out_shape=(vm((ro...  39.7 us

profile of v7, /device:TPU:1, one launch (start us, length us, event | category | flops | bytes accessed | tf_op | source)
XLA Modules:
  0.0 41.0 jit_solution(3045439498975454820)
XLA Ops:
  0.6 39.7 %shard_map.58 = (bf16[32,128]{1,0:T(8,128)(2,1)S(1)}, f32[2,32,128]{2,1,0:T(8,128)S(1)}, f32[128,128]{1,0:T(8,128)S(1)}) custom-call(bf16[32,128]{1,0:T(8,128)(2,1)} %x_ref.1, bf16[8192,128]{1,0:T(8,128)(2,1)} %basis_ref.1, bf16[128,128]{1,0:T(8,128)(2,1)} %map_ref.1), custom_call_target="tpu_custom_call" | custom-call | tf_op jit(solution)/shard_map/pallas_call | solution.py:306
  40.4 0.7 %shard_map.59 = (bf16[32,128]{1,0:T(8,128)(2,1)}, f32[8192]{0:T(1024)}, f32[128,128]{1,0:T(8,128)}) custom-call(bf16[32,128]{1,0:T(8,128)(2,1)S(1)} %get-tuple-element.6.q_in, f32[8192]{0:T(1024)S(1)} %bitcast.1, f32[128,128]{1,0:T(8,128)S(1)} %get-tuple-element.8.g_in), custom_call_target="tpu_custom_call" | custom-call | tf_op jit(solution)/shard_map/pallas_call | solution.py:345
